TPU v7x, 256 devices: a whole 4x4x8 slice. The times are simulated.
256 devices in a mesh: tile: 64 (over z, y, core), tm: 4 (over x).
Axes of the slice: x: 4, y: 4, z: 8, core: 2. Of those that a mesh axis runs over, the one named last changes fastest.
Arguments:
- latent: bfloat16 [12, 192, 1024], P('tm', 'tile'), may hold values from -56 to 56
- conv_in_weight: bfloat16 [3, 3, 3, 16, 384], replicated, may hold values from -0.3125 to 0.3125
- conv_in_bias: float32 [384], replicated, may hold values from -3 to 3
- first_gain: float32 [384], replicated, may hold values from 0.25 to 1.75
- conv_weight: bfloat16 [3, 3, 3, 384, 384], replicated, may hold values from -0.0625 to 0.0625
- conv_bias: float32 [384], replicated, may hold values from -3 to 3
- up_weight: bfloat16 [3, 3, 384, 192], replicated, may hold values from -0.109375 to 0.109375
- up_bias: float32 [192], replicated, may hold values from -3 to 3
Outputs:
- upsampled: bfloat16 [12, 64, 16, 48, 192], P('tm', 'tile')
All inputs are finite; a program needn't handle non-finite values.
Results may differ from a plain program's by a relative error of at most 0.0065.
Values may be sent and summed in bfloat16 or wider, within the bound.
No kernel may reach another device: no remote copies, remote signals or barrier semaphores. Data moves between devices by JAX's collectives and lax.ppermute only.
A program may use at most 64 MiB of HBM per device.

v0:
```python
import jax
import jax.numpy as jnp
from jax import lax
from jax.sharding import PartitionSpec as P

LAT_C = 16
HL = 8
WL = 24


def passed_along(value, axis, steps):
    count = lax.axis_size(axis)
    first, last = (max(0, -steps), min(count, count - steps))
    return lax.ppermute(value, axis, [(source, source + steps) for source in range(first, last)])


def add_rim(field, margin, columns):
    column = lax.axis_index("tile") % columns
    margins = []
    for offset, border, usable in (
        (1, field[:, :, -margin:], column > 0),
        (-1, field[:, :, :margin], column < columns - 1),
    ):
        arrived = passed_along(border, "tile", offset)
        margins.append(jnp.where(usable, arrived, jnp.zeros_like(arrived)))
    widened = jnp.concatenate([margins[0], field, margins[1]], axis=2)
    bands = []
    for offset, border in ((columns, widened[:, -margin:]), (-columns, widened[:, :margin])):
        bands.append(passed_along(border, "tile", offset))
    return jnp.concatenate([bands[0], widened, bands[1]], axis=1)


def convolve(extended, weight):
    time_taps = weight.shape[0]
    frames = extended.shape[0] - time_taps + 1
    height = extended.shape[1] - 2
    breadth = extended.shape[2] - 2
    in_channels = extended.shape[3]
    out_channels = weight.shape[4]
    summed = jnp.zeros((frames, height, breadth, out_channels), jnp.float32)
    for time_tap in range(time_taps):
        for row_tap in range(3):
            window = extended[time_tap : time_tap + frames, row_tap : row_tap + height]
            stacked = jnp.concatenate(
                [window[:, :, col_tap : col_tap + breadth] for col_tap in range(3)], axis=3
            )
            kernel = weight[time_tap, row_tap].reshape(3 * in_channels, out_channels)
            summed = summed + jnp.einsum(
                "fhwc,cd->fhwd", stacked, kernel, preferred_element_type=jnp.float32
            )
    return summed


def activate(field, gain_vector):
    values = field.astype(jnp.float32)
    scaling = lax.rsqrt(jnp.mean(values * values, axis=-1, keepdims=True) + 1e-06)
    return jax.nn.silu(values * scaling * gain_vector).astype(jnp.bfloat16)


def on_device(
    latent, conv_in_weight, conv_in_bias, first_gain, conv_weight, conv_bias, up_weight, up_bias
):
    frames = latent.shape[0]
    tile_count = lax.axis_size("tile")
    columns = min(8, tile_count // 2)
    pieces = latent.reshape(frames, latent.shape[1], tile_count, LAT_C)
    moved = lax.all_to_all(pieces, "tile", split_axis=2, concat_axis=1, tiled=True)
    own_latent = moved.reshape(frames, HL, WL, LAT_C)
    prior = passed_along(own_latent[-2:], "tm", 1)
    stacked_latent = jnp.concatenate([prior, own_latent], axis=0)
    latent_ext = add_rim(stacked_latent, 1, columns)
    start = (convolve(latent_ext, conv_in_weight) + conv_in_bias).astype(jnp.bfloat16)
    active = activate(start, first_gain)
    carried = passed_along(active[-2:], "tm", 1)
    active = jnp.concatenate([carried, active], axis=0)
    active = add_rim(active, 1, columns)
    hidden = (start.astype(jnp.float32) + convolve(active, conv_weight) + conv_bias).astype(
        jnp.bfloat16
    )
    hidden_ext = add_rim(hidden, 1, columns)
    doubled = jnp.repeat(jnp.repeat(hidden_ext, 2, axis=1), 2, axis=2)[:, 1:-1, 1:-1]
    result = (convolve(doubled, up_weight[None]) + up_bias).astype(jnp.bfloat16)
    return result.reshape(frames, 1, 2 * HL, 2 * WL, result.shape[3])


def solution(mesh):
    return jax.shard_map(
        on_device,
        mesh=mesh,
        in_specs=(P("tm", "tile", None), P(), P(), P(), P(), P(), P(), P()),
        out_specs=P("tm", "tile", None, None, None),
        check_vma=False,
    )
```

profile of v0, /device:TPU:102, one launch (start us, length us, event | category | flops | bytes accessed | tf_op | source)
XLA Modules:
  0.0 133.3 jit_solution(10314951593424221838)
XLA Ops:
  1.1 20.9 %all_to_all.15 = bf16[3,3,64,16]{3,1,0,2:T(4,128)(2,1)S(1)} all-to-all(bf16[3,3,64,16]{3,1,0,2:T(4,128)(2,1)S(1)} %copy.21), channel_id=1, replica_groups=mesh['tile'=64,'tm'=4] {'tile'}, dimensions={2} | all-to-all | bytes 36864 | tf_op jit(solution)/shard_map/all_to_all | solution.py:67
  22.1 1.3 collective-permute-start
  23.6 5.0 %collective-permute-done = bf16[2,8,24,16]{3,2,1,0:T(8,128)(2,1)S(1)} collective-permute-done((bf16[2,8,24,16]{3,2,1,0:T(8,128)(2,1)S(1)}, bf16[2,8,24,16]{3,2,1,0:T(8,128)(2,1)S(1)}, u32[]{:S(2)}, u32[]{:S(2)}) %collective-permute-start) | collective-permute-done | bytes 12320 | tf_op jit(solution)/shard_map/ppermute | solution.py:14
  28.8 1.9 %collective-permute-start.2 = (bf16[5,8,1,16]{3,2,1,0:T(2,128)(2,1)S(1)}, bf16[5,8,1,16]{3,2,1,0:T(2,128)(2,1)S(1)}, u32[]{:S(2)}, u32[]{:S(2)}) collective-permute-start(bf16[5,8,1,16]{3,2,1,0:T(2,128)(2,1)S(1)} %get-tuple-element.102), channel_id=1, source_target_pairs={{4,0},{8,4},{12,8},{16,12},{20,16},{24,20},{28,24},{32,28},{36,32}... | collective-permute-start | bytes 3848 | tf_op jit(solution)/shard_map/ppermute | solution.py:14
  30.8 2.4 %collective-permute-start.1 = (bf16[5,8,1,16]{3,2,1,0:T(2,128)(2,1)S(1)}, bf16[5,8,1,16]{3,2,1,0:T(2,128)(2,1)S(1)}, u32[]{:S(2)}, u32[]{:S(2)}) collective-permute-start(bf16[5,8,1,16]{3,2,1,0:T(2,128)(2,1)S(1)} %get-tuple-element.101), channel_id=1, source_target_pairs={{0,4},{4,8},{8,12},{12,16},{16,20},{20,24},{24,28},{28,32},{32,36}... | collective-permute-start | bytes 3848 | tf_op jit(solution)/shard_map/ppermute | solution.py:14
  33.2 4.8 %collective-permute-done.1 = bf16[5,8,1,16]{3,2,1,0:T(2,128)(2,1)S(1)} collective-permute-done((bf16[5,8,1,16]{3,2,1,0:T(2,128)(2,1)S(1)}, bf16[5,8,1,16]{3,2,1,0:T(2,128)(2,1)S(1)}, u32[]{:S(2)}, u32[]{:S(2)}) %collective-permute-start.1) | collective-permute-done | bytes 1312 | tf_op jit(solution)/shard_map/ppermute | solution.py:14
  38.0 4.9 %collective-permute-start.3 = (bf16[5,1,26,16]{3,2,1,0:T(8,128)(2,1)S(1)}, bf16[5,1,26,16]{3,2,1,0:T(8,128)(2,1)S(1)}, u32[]{:S(2)}, u32[]{:S(2)}) collective-permute-start(bf16[5,1,26,16]{3,2,1,0:T(8,128)(2,1)S(1)} %get-tuple-element.92), channel_id=1, source_target_pairs={{0,32},{4,36},{8,40},{12,44},{16,48},{20,52},{24,56},{28,60},{32,6... | collective-permute-start | bytes 12488 | tf_op jit(solution)/shard_map/ppermute | solution.py:14
  43.0 1.9 %collective-permute-start.4 = (bf16[5,1,26,16]{3,2,1,0:T(8,128)(2,1)S(1)}, bf16[5,1,26,16]{3,2,1,0:T(8,128)(2,1)S(1)}, u32[]{:S(2)}, u32[]{:S(2)}) collective-permute-start(bf16[5,1,26,16]{3,2,1,0:T(8,128)(2,1)S(1)} %get-tuple-element.91), channel_id=1, source_target_pairs={{32,0},{36,4},{40,8},{44,12},{48,16},{52,20},{56,24},{60,28},{64,3... | collective-permute-start | bytes 12488 | tf_op jit(solution)/shard_map/ppermute | solution.py:14
  45.2 4.9 %collective-permute-done.4 = bf16[5,1,26,16]{3,2,1,0:T(8,128)(2,1)S(1)} collective-permute-done((bf16[5,1,26,16]{3,2,1,0:T(8,128)(2,1)S(1)}, bf16[5,1,26,16]{3,2,1,0:T(8,128)(2,1)S(1)}, u32[]{:S(2)}, u32[]{:S(2)}) %collective-permute-start.4) | collective-permute-done | bytes 4192 | tf_op jit(solution)/shard_map/ppermute | solution.py:14
  54.8 1.3 collective-permute-start.5
  56.1 1.2 fusion.197
  57.3 6.1 %collective-permute-done.5 = bf16[2,8,24,384]{3,2,1,0:T(8,128)(2,1)S(1)} collective-permute-done((bf16[2,8,24,384]{3,2,1,0:T(8,128)(2,1)S(1)}, bf16[2,8,24,384]{3,2,1,0:T(8,128)(2,1)S(1)}, u32[]{:S(2)}, u32[]{:S(2)}) %collective-permute-start.5) | collective-permute-done | bytes 294944 | tf_op jit(solution)/shard_map/ppermute | solution.py:14
  63.5 1.9 %collective-permute-start.7 = (bf16[5,8,1,384]{3,2,1,0:T(2,128)(2,1)S(1)}, bf16[5,8,1,384]{3,2,1,0:T(2,128)(2,1)S(1)}, u32[]{:S(2)}, u32[]{:S(2)}) collective-permute-start(bf16[5,8,1,384]{3,2,1,0:T(2,128)(2,1)S(1)} %get-tuple-element.57), channel_id=1, source_target_pairs={{4,0},{8,4},{12,8},{16,12},{20,16},{24,20},{28,24},{32,28},{36,32}... | collective-permute-start | bytes 92168 | tf_op jit(solution)/shard_map/ppermute | solution.py:14
  65.4 2.4 %collective-permute-start.6 = (bf16[5,8,1,384]{3,2,1,0:T(2,128)(2,1)S(1)}, bf16[5,8,1,384]{3,2,1,0:T(2,128)(2,1)S(1)}, u32[]{:S(2)}, u32[]{:S(2)}) collective-permute-start(bf16[5,8,1,384]{3,2,1,0:T(2,128)(2,1)S(1)} %get-tuple-element.56), channel_id=1, source_target_pairs={{0,4},{4,8},{8,12},{12,16},{16,20},{20,24},{24,28},{28,32},{32,36}... | collective-permute-start | bytes 92168 | tf_op jit(solution)/shard_map/ppermute | solution.py:14
  68.0 5.1 %collective-permute-done.6 = bf16[5,8,1,384]{3,2,1,0:T(2,128)(2,1)S(1)} collective-permute-done((bf16[5,8,1,384]{3,2,1,0:T(2,128)(2,1)S(1)}, bf16[5,8,1,384]{3,2,1,0:T(2,128)(2,1)S(1)}, u32[]{:S(2)}, u32[]{:S(2)}) %collective-permute-start.6) | collective-permute-done | bytes 30752 | tf_op jit(solution)/shard_map/ppermute | solution.py:14
  74.3 3.0 %collective-permute-start.8 = (bf16[5,1,26,384]{3,2,1,0:T(8,128)(2,1)S(1)}, bf16[5,1,26,384]{3,2,1,0:T(8,128)(2,1)S(1)}, u32[]{:S(2)}, u32[]{:S(2)}) collective-permute-start(bf16[5,1,26,384]{3,2,1,0:T(8,128)(2,1)S(1)} %get-tuple-element.53), channel_id=1, source_target_pairs={{0,32},{4,36},{8,40},{12,44},{16,48},{20,52},{24,56},{28,60},{32,6... | collective-permute-start | bytes 299528 | tf_op jit(solution)/shard_map/ppermute | solution.py:14
  77.4 3.0 %collective-permute-start.9 = (bf16[5,1,26,384]{3,2,1,0:T(8,128)(2,1)S(1)}, bf16[5,1,26,384]{3,2,1,0:T(8,128)(2,1)S(1)}, u32[]{:S(2)}, u32[]{:S(2)}) collective-permute-start(bf16[5,1,26,384]{3,2,1,0:T(8,128)(2,1)S(1)} %get-tuple-element.52), channel_id=1, source_target_pairs={{32,0},{36,4},{40,8},{44,12},{48,16},{52,20},{56,24},{60,28},{64,3... | collective-permute-start | bytes 299528 | tf_op jit(solution)/shard_map/ppermute | solution.py:14
  83.3 2.1 %collective-permute-done.9 = bf16[5,1,26,384]{3,2,1,0:T(8,128)(2,1)S(1)} collective-permute-done((bf16[5,1,26,384]{3,2,1,0:T(8,128)(2,1)S(1)}, bf16[5,1,26,384]{3,2,1,0:T(8,128)(2,1)S(1)}, u32[]{:S(2)}, u32[]{:S(2)}) %collective-permute-start.9) | collective-permute-done | bytes 99872 | tf_op jit(solution)/shard_map/ppermute | solution.py:14
  91.1 1.1 fusion.105
  93.3 1.9 %collective-permute-start.10 = (bf16[3,8,1,384]{3,2,1,0:T(2,128)(2,1)S(1)}, bf16[3,8,1,384]{3,2,1,0:T(2,128)(2,1)S(1)}, u32[]{:S(2)}, u32[]{:S(2)}) collective-permute-start(bf16[3,8,1,384]{3,2,1,0:T(2,128)(2,1)S(1)} %get-tuple-element.60), channel_id=1, source_target_pairs={{0,4},{4,8},{8,12},{12,16},{16,20},{20,24},{24,28},{28,32},{32,36}... | collective-permute-start | bytes 55304 | tf_op jit(solution)/shard_map/ppermute | solution.py:14
  95.2 5.8 %collective-permute-start.11 = (bf16[3,8,1,384]{3,2,1,0:T(2,128)(2,1)S(1)}, bf16[3,8,1,384]{3,2,1,0:T(2,128)(2,1)S(1)}, u32[]{:S(2)}, u32[]{:S(2)}) collective-permute-start(bf16[3,8,1,384]{3,2,1,0:T(2,128)(2,1)S(1)} %get-tuple-element.61), channel_id=1, source_target_pairs={{4,0},{8,4},{12,8},{16,12},{20,16},{24,20},{28,24},{32,28},{36,32}... | collective-permute-start | bytes 55304 | tf_op jit(solution)/shard_map/ppermute | solution.py:14
  101.0 1.6 %collective-permute-done.11 = bf16[3,8,1,384]{3,2,1,0:T(2,128)(2,1)S(1)} collective-permute-done((bf16[3,8,1,384]{3,2,1,0:T(2,128)(2,1)S(1)}, bf16[3,8,1,384]{3,2,1,0:T(2,128)(2,1)S(1)}, u32[]{:S(2)}, u32[]{:S(2)}) %collective-permute-start.11) | collective-permute-done | bytes 18464 | tf_op jit(solution)/shard_map/ppermute | solution.py:14
  102.7 3.4 %collective-permute-start.12 = (bf16[3,1,26,384]{3,2,1,0:T(8,128)(2,1)S(1)}, bf16[3,1,26,384]{3,2,1,0:T(8,128)(2,1)S(1)}, u32[]{:S(2)}, u32[]{:S(2)}) collective-permute-start(bf16[3,1,26,384]{3,2,1,0:T(8,128)(2,1)S(1)} %get-tuple-element.58), channel_id=1, source_target_pairs={{0,32},{4,36},{8,40},{12,44},{16,48},{20,52},{24,56},{28,60},{32,6... | collective-permute-start | bytes 179720 | tf_op jit(solution)/shard_map/ppermute | solution.py:14
  106.1 2.7 %collective-permute-start.13 = (bf16[3,1,26,384]{3,2,1,0:T(8,128)(2,1)S(1)}, bf16[3,1,26,384]{3,2,1,0:T(8,128)(2,1)S(1)}, u32[]{:S(2)}, u32[]{:S(2)}) collective-permute-start(bf16[3,1,26,384]{3,2,1,0:T(8,128)(2,1)S(1)} %get-tuple-element.59), channel_id=1, source_target_pairs={{32,0},{36,4},{40,8},{44,12},{48,16},{52,20},{56,24},{60,28},{64,3... | collective-permute-start | bytes 179720 | tf_op jit(solution)/shard_map/ppermute | solution.py:14
  109.3 1.1 reshape.53
  112.0 1.5 %collective-permute-done.13 = bf16[3,1,26,384]{3,2,1,0:T(8,128)(2,1)S(1)} collective-permute-done((bf16[3,1,26,384]{3,2,1,0:T(8,128)(2,1)S(1)}, bf16[3,1,26,384]{3,2,1,0:T(8,128)(2,1)S(1)}, u32[]{:S(2)}, u32[]{:S(2)}) %collective-permute-start.13) | collective-permute-done | bytes 59936 | tf_op jit(solution)/shard_map/ppermute | solution.py:14
  114.0 2.8 %broadcast_in_dim.7 = bf16[3,20,26,2,384]{4,3,2,1,0:T(2,128)(2,1)} broadcast(bf16[3,20,26,384]{3,2,1,0:T(8,128)(2,1)S(1)} %bitcast.137), dimensions={0,1,2,4} | broadcast | bytes 3594240 | tf_op jit(solution)/shard_map/broadcast_in_dim | solution.py:81
  116.8 5.1 %reshape.32 = bf16[3,20,52,384]{3,2,1,0:T(8,128)(2,1)S(1)} reshape(bf16[3,20,26,2,384]{4,3,2,1,0:T(2,128)(2,1)} %broadcast_in_dim.7) | data formatting | bytes 4792320 | tf_op jit(solution)/shard_map/reshape | solution.py:81
  122.0 4.9 %fusion.198 = (bf16[3,16,48,384]{3,2,1,0:T(8,128)(2,1)S(1)}, bf16[3,16,48,384]{3,2,1,0:T(8,128)(2,1)S(1)}, bf16[3,16,48,384]{3,2,1,0:T(8,128)(2,1)S(1)}, bf16[3,...) fusion(bf16[3,20,52,384]{3,2,1,0:T(8,128)(2,1)S(1)} %reshape.32), kind=kLoop, calls=%fused_computation.222 | loop fusion | bytes 31850496 | tf_op jit(solution)/shard_map/slice | solution.py:45
  126.9 1.7 %fusion.6 = f32[3,16,48,192]{3,2,1,0:T(8,128)S(1)} fusion(bf16[3,16,48,384]{3,2,1,0:T(8,128)(2,1)S(1)} %get-tuple-element.18, bf16[3,16,48,384]{3,2,1,0:T(8,128)(2,1)S(1)} %get-tuple-element.19, bf16[3,16,48,384]{3,2,1,0:T(8,128)(2,1)S(1)} %get-tuple-element.14, bf16[1152,192,1,1]{0,1,2,3:T(8,128)(2,1)S(1)} %copy-done.1), kind=kOutput, calls=%fused_computation.6 | convolution fusion | flops 1035141120 | bytes 7520256 | tf_op jit(solution)/shard_map/fhwc,cd->fhwd/dot_general | solution.py:48
  128.7 1.8 %fusion = f32[3,16,48,192]{3,2,1,0:T(8,128)S(1)} fusion(bf16[3,16,48,384]{3,2,1,0:T(8,128)(2,1)S(1)} %get-tuple-element.20, bf16[3,16,48,384]{3,2,1,0:T(8,128)(2,1)S(1)} %get-tuple-element.21, bf16[3,16,48,384]{3,2,1,0:T(8,128)(2,1)S(1)} %get-tuple-element.22, bf16[1152,192,1,1]{0,1,2,3:T(8,128)(2,1)S(1)} %reshape.52), kind=kOutput, calls=%fused_computation | convolution fusion | flops 1035141120 | bytes 7520256 | tf_op jit(solution)/shard_map/fhwc,cd->fhwd/dot_general | solution.py:48
  130.4 2.9 %fusion.20 = bf16[3,1,16,48,192]{4,3,2,1,0:T(8,128)(2,1)} fusion(bf16[3,16,48,384]{3,2,1,0:T(8,128)(2,1)S(1)} %get-tuple-element.15, bf16[3,16,48,384]{3,2,1,0:T(8,128)(2,1)S(1)} %get-tuple-element.16, bf16[3,16,48,384]{3,2,1,0:T(8,128)(2,1)S(1)} %get-tuple-element.17, f32[3,16,48,192]{3,2,1,0:T(8,128)S(1)} %fusion, f32[3,16,48,192]{3,2,1,0:T(8,128)S(1)} %fusion.6, ...), kind=kOutput, calls=%fused_computation.19 | convolution fusion | flops 1036910592 | bytes 10175232 | tf_op jit(solution)/shard_map/fhwc,cd->fhwd/dot_general | solution.py:48
  (85 shorter events, 20.2 us)
Async XLA Ops:
  0.0 30.7 %copy-start.2 = (bf16[3,3,3,16,384]{4,3,2,1,0:T(8,128)(2,1)S(1)}, bf16[3,3,3,16,384]{4,3,2,1,0:T(8,128)(2,1)}, u32[]{:S(2)}) copy-start(bf16[3,3,3,16,384]{4,3,2,1,0:T(8,128)(2,1)} %param.9) | copy-start | bytes 995332
  22.1 6.5 %collective-permute-start = (bf16[2,8,24,16]{3,2,1,0:T(8,128)(2,1)S(1)}, bf16[2,8,24,16]{3,2,1,0:T(8,128)(2,1)S(1)}, u32[]{:S(2)}, u32[]{:S(2)}) collective-permute-start(bf16[2,8,24,16]{3,2,1,0:T(8,128)(2,1)S(1)} %copy.23), channel_id=1, source_target_pairs={{0,1},{1,2},{2,3},{4,5},{5,6},{6,7},{8,9},{9,10},{10,11},{12,13},{... | collective-permute-start | bytes 36872 | tf_op jit(solution)/shard_map/ppermute | solution.py:14
  28.8 4.4 %collective-permute-start.2 = (bf16[5,8,1,16]{3,2,1,0:T(2,128)(2,1)S(1)}, bf16[5,8,1,16]{3,2,1,0:T(2,128)(2,1)S(1)}, u32[]{:S(2)}, u32[]{:S(2)}) collective-permute-start(bf16[5,8,1,16]{3,2,1,0:T(2,128)(2,1)S(1)} %get-tuple-element.102), channel_id=1, source_target_pairs={{4,0},{8,4},{12,8},{16,12},{20,16},{24,20},{28,24},{32,28},{36,32}... | collective-permute-start | bytes 3848 | tf_op jit(solution)/shard_map/ppermute | solution.py:14
  30.8 7.2 %collective-permute-start.1 = (bf16[5,8,1,16]{3,2,1,0:T(2,128)(2,1)S(1)}, bf16[5,8,1,16]{3,2,1,0:T(2,128)(2,1)S(1)}, u32[]{:S(2)}, u32[]{:S(2)}) collective-permute-start(bf16[5,8,1,16]{3,2,1,0:T(2,128)(2,1)S(1)} %get-tuple-element.101), channel_id=1, source_target_pairs={{0,4},{4,8},{8,12},{12,16},{16,20},{20,24},{24,28},{28,32},{32,36}... | collective-permute-start | bytes 3848 | tf_op jit(solution)/shard_map/ppermute | solution.py:14
  38.0 7.1 %collective-permute-start.3 = (bf16[5,1,26,16]{3,2,1,0:T(8,128)(2,1)S(1)}, bf16[5,1,26,16]{3,2,1,0:T(8,128)(2,1)S(1)}, u32[]{:S(2)}, u32[]{:S(2)}) collective-permute-start(bf16[5,1,26,16]{3,2,1,0:T(8,128)(2,1)S(1)} %get-tuple-element.92), channel_id=1, source_target_pairs={{0,32},{4,36},{8,40},{12,44},{16,48},{20,52},{24,56},{28,60},{32,6... | collective-permute-start | bytes 12488 | tf_op jit(solution)/shard_map/ppermute | solution.py:14
  43.0 7.1 %collective-permute-start.4 = (bf16[5,1,26,16]{3,2,1,0:T(8,128)(2,1)S(1)}, bf16[5,1,26,16]{3,2,1,0:T(8,128)(2,1)S(1)}, u32[]{:S(2)}, u32[]{:S(2)}) collective-permute-start(bf16[5,1,26,16]{3,2,1,0:T(8,128)(2,1)S(1)} %get-tuple-element.91), channel_id=1, source_target_pairs={{32,0},{36,4},{40,8},{44,12},{48,16},{52,20},{56,24},{60,28},{64,3... | collective-permute-start | bytes 12488 | tf_op jit(solution)/shard_map/ppermute | solution.py:14
  52.0 4.1 %slice-start = ((s8[7962624]{0:T(1024)(128)(4,1)}), s8[4194304]{0:T(1024)(128)(4,1)S(1)}, s32[]{:S(2)}) async-start(s8[7962624]{0:T(1024)(128)(4,1)} %bitcast.135), calls=%async_computation.1 | async-start | bytes 8388608
  53.1 0.8 copy-start.4
  53.1 3.0 %slice-start.1 = ((s8[7962624]{0:T(1024)(128)(4,1)}), s8[3768320]{0:T(1024)(128)(4,1)S(1)}, s32[]{:S(2)}) async-start(s8[7962624]{0:T(1024)(128)(4,1)} %bitcast.135), calls=%async_computation.2 | async-start | bytes 7536640
  53.5 0.9 copy-start.3
  54.8 8.6 %collective-permute-start.5 = (bf16[2,8,24,384]{3,2,1,0:T(8,128)(2,1)S(1)}, bf16[2,8,24,384]{3,2,1,0:T(8,128)(2,1)S(1)}, u32[]{:S(2)}, u32[]{:S(2)}) collective-permute-start(bf16[2,8,24,384]{3,2,1,0:T(8,128)(2,1)S(1)} %slice.539), channel_id=1, source_target_pairs={{0,1},{1,2},{2,3},{4,5},{5,6},{6,7},{8,9},{9,10},{10,11},{12,13},{... | collective-permute-start | bytes 884744 | tf_op jit(solution)/shard_map/ppermute | solution.py:14
  63.5 4.4 %collective-permute-start.7 = (bf16[5,8,1,384]{3,2,1,0:T(2,128)(2,1)S(1)}, bf16[5,8,1,384]{3,2,1,0:T(2,128)(2,1)S(1)}, u32[]{:S(2)}, u32[]{:S(2)}) collective-permute-start(bf16[5,8,1,384]{3,2,1,0:T(2,128)(2,1)S(1)} %get-tuple-element.57), channel_id=1, source_target_pairs={{4,0},{8,4},{12,8},{16,12},{20,16},{24,20},{28,24},{32,28},{36,32}... | collective-permute-start | bytes 92168 | tf_op jit(solution)/shard_map/ppermute | solution.py:14
  65.4 7.7 %collective-permute-start.6 = (bf16[5,8,1,384]{3,2,1,0:T(2,128)(2,1)S(1)}, bf16[5,8,1,384]{3,2,1,0:T(2,128)(2,1)S(1)}, u32[]{:S(2)}, u32[]{:S(2)}) collective-permute-start(bf16[5,8,1,384]{3,2,1,0:T(2,128)(2,1)S(1)} %get-tuple-element.56), channel_id=1, source_target_pairs={{0,4},{4,8},{8,12},{12,16},{16,20},{20,24},{24,28},{28,32},{32,36}... | collective-permute-start | bytes 92168 | tf_op jit(solution)/shard_map/ppermute | solution.py:14
  74.3 8.9 %collective-permute-start.8 = (bf16[5,1,26,384]{3,2,1,0:T(8,128)(2,1)S(1)}, bf16[5,1,26,384]{3,2,1,0:T(8,128)(2,1)S(1)}, u32[]{:S(2)}, u32[]{:S(2)}) collective-permute-start(bf16[5,1,26,384]{3,2,1,0:T(8,128)(2,1)S(1)} %get-tuple-element.53), channel_id=1, source_target_pairs={{0,32},{4,36},{8,40},{12,44},{16,48},{20,52},{24,56},{28,60},{32,6... | collective-permute-start | bytes 299528 | tf_op jit(solution)/shard_map/ppermute | solution.py:14
  77.4 8.0 %collective-permute-start.9 = (bf16[5,1,26,384]{3,2,1,0:T(8,128)(2,1)S(1)}, bf16[5,1,26,384]{3,2,1,0:T(8,128)(2,1)S(1)}, u32[]{:S(2)}, u32[]{:S(2)}) collective-permute-start(bf16[5,1,26,384]{3,2,1,0:T(8,128)(2,1)S(1)} %get-tuple-element.52), channel_id=1, source_target_pairs={{32,0},{36,4},{40,8},{44,12},{48,16},{52,20},{56,24},{60,28},{64,3... | collective-permute-start | bytes 299528 | tf_op jit(solution)/shard_map/ppermute | solution.py:14
  91.1 1.1 copy-start.5
  92.2 16.5 %copy-start = (bf16[3,3,384,192]{2,3,1,0:T(8,128)(2,1)S(1)}, bf16[3,3,384,192]{2,3,1,0:T(8,128)(2,1)}, u32[]{:S(2)}) copy-start(bf16[3,3,384,192]{2,3,1,0:T(8,128)(2,1)} %param.14) | copy-start | bytes 3981316
  93.3 7.7 %collective-permute-start.10 = (bf16[3,8,1,384]{3,2,1,0:T(2,128)(2,1)S(1)}, bf16[3,8,1,384]{3,2,1,0:T(2,128)(2,1)S(1)}, u32[]{:S(2)}, u32[]{:S(2)}) collective-permute-start(bf16[3,8,1,384]{3,2,1,0:T(2,128)(2,1)S(1)} %get-tuple-element.60), channel_id=1, source_target_pairs={{0,4},{4,8},{8,12},{12,16},{16,20},{20,24},{24,28},{28,32},{32,36}... | collective-permute-start | bytes 55304 | tf_op jit(solution)/shard_map/ppermute | solution.py:14
  95.2 7.4 %collective-permute-start.11 = (bf16[3,8,1,384]{3,2,1,0:T(2,128)(2,1)S(1)}, bf16[3,8,1,384]{3,2,1,0:T(2,128)(2,1)S(1)}, u32[]{:S(2)}, u32[]{:S(2)}) collective-permute-start(bf16[3,8,1,384]{3,2,1,0:T(2,128)(2,1)S(1)} %get-tuple-element.61), channel_id=1, source_target_pairs={{4,0},{8,4},{12,8},{16,12},{20,16},{24,20},{28,24},{32,28},{36,32}... | collective-permute-start | bytes 55304 | tf_op jit(solution)/shard_map/ppermute | solution.py:14
  102.7 9.3 %collective-permute-start.12 = (bf16[3,1,26,384]{3,2,1,0:T(8,128)(2,1)S(1)}, bf16[3,1,26,384]{3,2,1,0:T(8,128)(2,1)S(1)}, u32[]{:S(2)}, u32[]{:S(2)}) collective-permute-start(bf16[3,1,26,384]{3,2,1,0:T(8,128)(2,1)S(1)} %get-tuple-element.58), channel_id=1, source_target_pairs={{0,32},{4,36},{8,40},{12,44},{16,48},{20,52},{24,56},{28,60},{32,6... | collective-permute-start | bytes 179720 | tf_op jit(solution)/shard_map/ppermute | solution.py:14
  106.1 7.5 %collective-permute-start.13 = (bf16[3,1,26,384]{3,2,1,0:T(8,128)(2,1)S(1)}, bf16[3,1,26,384]{3,2,1,0:T(8,128)(2,1)S(1)}, u32[]{:S(2)}, u32[]{:S(2)}) collective-permute-start(bf16[3,1,26,384]{3,2,1,0:T(8,128)(2,1)S(1)} %get-tuple-element.59), channel_id=1, source_target_pairs={{32,0},{36,4},{40,8},{44,12},{48,16},{52,20},{56,24},{60,28},{64,3... | collective-permute-start | bytes 179720 | tf_op jit(solution)/shard_map/ppermute | solution.py:14
  122.0 4.9 %copy-start.1 = (bf16[1152,192,1,1]{0,1,2,3:T(8,128)(2,1)S(1)}, bf16[1152,192,1,1]{0,1,2,3:T(8,128)(2,1)}, u32[]{:S(2)}) copy-start(bf16[1152,192,1,1]{0,1,2,3:T(8,128)(2,1)} %reshape.53) | copy-start | bytes 1327108
  128.6 1.8 %copy-start.6 = (f32[192]{0:T(256)S(1)}, f32[192]{0:T(256)}, u32[]{:S(2)}) copy-start(f32[192]{0:T(256)} %param.15) | copy-start | bytes 2308
where the time goes:
time: 134 us; the launch traced here: 133 us
  starting transfers between devices  37.8 us (28%)
  waiting for transfers between devices  31.1 us (23%)
  local copies, waits for them, and re-layouts  21.1 us (16%)
  blocking collectives  20.9 us (16%)
  matrix products  18.4 us (14%)
  other arithmetic  3.26 us (2%)
    ppermute x14, starting transfers between devices, passed_along(): lax.ppermute(value, axis, [(source, source + steps) for source in range(f...  37.8 us
    ppermute x14, waiting for transfers between devices, passed_along(): lax.ppermute(value, axis, [(source, source + steps) for source in range(f...  31.1 us
    all_to_all x1, blocking collectives, on_device(): lax.all_to_all(pieces, 'tile', split_axis=2, concat_axis=1, tiled=True)  20.9 us
    dot_general x21, matrix products, convolve(): jnp.einsum('fhwc,cd->fhwd', stacked, kernel, preferred_element_type=jnp.f...  18.4 us
    slice x6, local copies, waits for them, and re-layouts, convolve(): window[:, :, col_tap:col_tap + breadth]  6.97 us
    reshape x1, local copies, waits for them, and re-layouts, on_device(): jnp.repeat(jnp.repeat(hidden_ext, 2, axis=1), 2, axis=2)[:, 1:-1, 1:-1]  5.14 us
    broadcast_in_dim x1, local copies, waits for them, and re-layouts, on_device(): jnp.repeat(jnp.repeat(hidden_ext, 2, axis=1), 2, axis=2)[:, 1:-1, 1:-1]  2.81 us
  transfers between devices with their start and end apart: 14, of which 8 were waited for; matrix products, arithmetic and copies ran while one was open for 6% of the time, Pallas kernels for 0%

commit v1 on v0

v1 whole, which is shorter than its diff:
```python
import jax
import jax.numpy as jnp
from jax import lax
from jax.experimental import pallas as pl
from jax.experimental.pallas import tpu as pltpu
from jax.sharding import PartitionSpec as P

LAT_C = 16
C = 384
C_UP = 192
HL = 8
WL = 24
GRID = 8
S = 32
LANE_OF_FRAME = (48, 0, 16, 32, 64, 80, 96)


def exchange(latent):
    tiles = latent.reshape(3, 3, GRID, GRID, LAT_C).transpose(2, 3, 1, 0, 4)
    tiles = jnp.concatenate([tiles, tiles[:, :, :, 2:]], axis=3).reshape(GRID, GRID, 3 * 64)
    index = lax.axis_index("tile")
    r, g = index // GRID, index % GRID
    side = jnp.where(g < 4, jnp.roll(tiles, -1, axis=1), jnp.roll(tiles, 1, axis=1))
    wide = jnp.concatenate([tiles, side], axis=2)
    other = jnp.where(r < 4, jnp.roll(wide, -1, axis=0), jnp.roll(wide, 1, axis=0))
    pieces = jnp.stack([wide, other], axis=2).reshape(1, GRID * GRID, 2, 6 * 64)
    count = lax.axis_size("tm")
    send = jnp.broadcast_to(pieces, (count, GRID * GRID, 2, 6 * 64)).reshape(count * GRID * GRID, 2, 6 * 64)
    moved = lax.all_to_all(send, ("tm", "tile"), split_axis=0, concat_axis=0, tiled=True)
    return moved.reshape(count * GRID * GRID * 2, 6 * 64)


def prepare(w1_ref, w2_ref, up_ref, t1_ref, t2_ref, tu_ref, sem):
    copies = [
        pltpu.make_async_copy(w2_ref.at[dt], t2_ref.at[:, (2 - dt) * C : (3 - dt) * C], sem.at[dt])
        for dt in range(3)
    ]
    for copy in copies:
        copy.start()
    t1_ref[...] = jnp.zeros(t1_ref.shape, t1_ref.dtype)
    for tap in range(9):
        for frame in range(5):
            for dt in range(3):
                row = tap * 128 + LANE_OF_FRAME[frame + dt]
                source = (dt * 9 + tap) * LAT_C
                t1_ref[row : row + LAT_C, frame * C : (frame + 1) * C] = w1_ref[source : source + LAT_C, :]
    tu_ref[...] = jnp.zeros(tu_ref.shape, tu_ref.dtype)
    groups = (((0,), (1, 2)), ((0, 1), (2,)))
    for py in range(2):
        for px in range(2):
            for ey in range(2):
                for ex in range(2):
                    total = None
                    for dy in groups[py][ey]:
                        for dx in groups[px][ex]:
                            part = up_ref[dy * 3 + dx].astype(jnp.float32)
                            total = part if total is None else total + part
                    row = (ey * 2 + ex) * C
                    tu_ref[py * 2 + px, row : row + C, 0:C_UP] = total.T.astype(jnp.bfloat16)
    for copy in copies:
        copy.wait()


def place(shape, dim):
    return lax.broadcasted_iota(jnp.int32, shape, dim)


def section(
    recv_ref, t1_ref, t2_ref, tu_ref, b1_ref, gain_ref, b2_ref, bu_ref, out_ref,
    x_ref, l1_ref, act_ref, la_ref, acc_ref, lh_ref, up_ref,
):
    x = lax.axis_index("tm")
    tile = lax.axis_index("tile")
    a, b = lax.div(tile, GRID), lax.rem(tile, GRID)
    f32, bf16 = jnp.float32, jnp.bfloat16

    blocks = []
    for d in range(3):
        first = pl.multiple_of(jnp.maximum(x - d, 0) * 128, 128)
        block = recv_ref[pl.ds(first, 128), :].astype(f32)
        blocks.append(jnp.where(x >= d, block, 0.0))
    lane = place((128, 128), 1)
    parts = []
    for j in range(3):
        now, before, older = [block[:, j * 128 : (j + 1) * 128] for block in blocks]
        past = jnp.where((lane & 63) >= 48, older, before)
        parts.append(jnp.where(lane < 64, past, pltpu.roll(now, 64, 1)))
        parts.append(jnp.where(lane < 64, pltpu.roll(past, 64, 1), now))
    rows = 14 * S
    stacked = jnp.concatenate(
        [parts[h * 3 + cell].astype(bf16) for cell in range(3) for h in range(2)], axis=0
    )
    row = place((rows, 768), 0)
    big_r, col = row >> 5, row & 31
    group = (col * 43) >> 7
    cell = col - 3 * group
    r = (big_r + 5) & 7
    g = (group + 7) & 7
    outer_r = jnp.where((big_r < 3) | (big_r >= 11), 1, 0)
    outer_g = jnp.where((group == 0) | (group == 9), 1, 0)
    source = cell * 256 + outer_g * 128 + r * 16 + g * 2 + outer_r
    frame_r = big_r + a * 8 - 3
    frame_c = col + b * 24 - 3
    inside = (frame_r >= 0) & (frame_r < 64) & (frame_c >= 0) & (frame_c < 192) & (col < 30)
    pick = jnp.where((place((rows, 768), 1) == source) & inside, 1.0, 0.0).astype(bf16)
    x_ref[0:rows, :] = jnp.dot(pick, stacked, preferred_element_type=f32)
    x_ref[rows : rows + 8, :] = jnp.zeros((8, 128), f32)
    for dx in range(3):
        l1_ref[:, dx * 128 : (dx + 1) * 128] = x_ref[pl.ds(dx, rows), :].astype(bf16)

    m1 = 12 * S
    lhs = jnp.concatenate([l1_ref[dy * S : dy * S + m1, :] for dy in range(3)], axis=1)
    position = place((m1, 1), 0)
    frame_r = (position >> 5) + a * 8 - 2
    frame_c = (position & 31) + b * 24 - 2
    inside = (frame_r >= 0) & (frame_r < 64) & (frame_c >= 0) & (frame_c < 192)
    m2 = 10 * S
    act_ref[m1 : m1 + 8, :] = jnp.zeros((8, C), f32)
    for frame in range(5):
        field = jnp.dot(lhs, t1_ref[:, frame * C : (frame + 1) * C], preferred_element_type=f32) + b1_ref[...]
        start = field.astype(bf16).astype(f32)
        if frame >= 2:
            act_ref[0:m1, :] = start
            acc_ref[:, (frame - 2) * C : (frame - 1) * C] = act_ref[pl.ds(S + 1, m2), :] + b2_ref[...]
        scaling = lax.rsqrt(jnp.mean(start * start, axis=1, keepdims=True) + 1e-06)
        value = start * scaling * gain_ref[...]
        value = value / (1.0 + jnp.exp(-value))
        keep = inside if frame >= 2 else inside & (x > 0)
        act_ref[0:m1, :] = jnp.where(keep, value, 0.0)
        for dx in range(3):
            la_ref[frame, :, dx * C : (dx + 1) * C] = act_ref[pl.ds(dx, m1), :].astype(bf16)

    for frame in range(5):
        lhs = jnp.concatenate([la_ref[frame, dy * S : dy * S + m2, :] for dy in range(3)], axis=1)
        low, high = max(0, frame - 2), min(2, frame)
        for t in range(low, high + 1):
            block = 2 - frame + t
            acc_ref[:, t * C : (t + 1) * C] += jnp.dot(
                lhs, t2_ref[:, block * C : (block + 1) * C], preferred_element_type=f32
            )

    position = place((m2, 1), 0)
    frame_r = (position >> 5) + a * 8 - 1
    frame_c = (position & 31) + b * 24 - 1
    inside = (frame_r >= 0) & (frame_r < 64) & (frame_c >= 0) & (frame_c < 192)
    m3 = 8 * S
    for t in range(3):
        act_ref[0:m2, :] = jnp.where(inside, acc_ref[:, t * C : (t + 1) * C], 0.0)
        for dx in range(3):
            lh_ref[:, dx * C : (dx + 1) * C] = act_ref[pl.ds(dx, m2), :].astype(bf16)
        for py in range(2):
            for px in range(2):
                lhs = jnp.concatenate(
                    [
                        lh_ref[(py + ey) * S : (py + ey) * S + m3, (px + ex) * C : (px + ex + 1) * C]
                        for ey in range(2)
                        for ex in range(2)
                    ],
                    axis=1,
                )
                phase = jnp.dot(lhs, tu_ref[py * 2 + px], preferred_element_type=f32) + bu_ref[...]
                for y in range(HL):
                    for part in range(2):
                        up_ref[part, 2 * y + py, pl.ds(px, WL, stride=2), :] = phase[
                            y * S : y * S + WL, part * 128 : (part + 1) * 128
                        ]
        out_ref[t, 0, :, :, 0:128] = up_ref[0].astype(bf16)
        out_ref[t, 0, :, :, 128:C_UP] = up_ref[1, :, :, 0 : C_UP - 128].astype(bf16)


def on_device(
    latent, conv_in_weight, conv_in_bias, first_gain, conv_weight, conv_bias, up_weight, up_bias
):
    vmem = pl.BlockSpec(memory_space=pltpu.VMEM)
    bf16, f32 = jnp.bfloat16, jnp.float32
    prepared = pl.pallas_call(
        prepare,
        out_shape=[
            pltpu.VMEM((9 * 128, 5 * C), bf16),
            pltpu.VMEM((9 * C, 3 * C), bf16),
            pltpu.VMEM((4, 4 * C, 256), bf16),
        ],
        in_specs=[vmem, pl.BlockSpec(memory_space=pl.ANY), vmem],
        out_specs=[vmem, vmem, vmem],
        scratch_shapes=[pltpu.SemaphoreType.DMA((3,))],
        compiler_params=pltpu.CompilerParams(vmem_limit_bytes=28 * 2**20),
        cost_estimate=pl.CostEstimate(flops=10**9, bytes_accessed=20_000_000, transcendentals=0),
        name="prepare",
    )(
        conv_in_weight.reshape(27 * LAT_C, C),
        conv_weight.reshape(3, 9 * C, C),
        up_weight.transpose(0, 1, 3, 2).reshape(9, C_UP, C),
    )
    received = exchange(latent)
    return pl.pallas_call(
        section,
        out_shape=jax.ShapeDtypeStruct((3, 1, 2 * HL, 2 * WL, C_UP), bf16),
        in_specs=[vmem] * 8,
        out_specs=vmem,
        scratch_shapes=[
            pltpu.VMEM((14 * S + 8, 128), f32),
            pltpu.VMEM((14 * S, 3 * 128), bf16),
            pltpu.VMEM((12 * S + 8, C), f32),
            pltpu.VMEM((5, 12 * S, 3 * C), bf16),
            pltpu.VMEM((10 * S, 3 * C), f32),
            pltpu.VMEM((10 * S, 3 * C), bf16),
            pltpu.VMEM((2, 2 * HL, 2 * WL, 128), f32),
        ],
        compiler_params=pltpu.CompilerParams(vmem_limit_bytes=36 * 2**20),
        cost_estimate=pl.CostEstimate(flops=8 * 10**9, bytes_accessed=2_000_000, transcendentals=10**6),
        name="section",
    )(
        received,
        *prepared,
        conv_in_bias.reshape(1, C),
        first_gain.reshape(1, C),
        conv_bias.reshape(1, C),
        jnp.pad(up_bias, (0, 256 - C_UP)).reshape(1, 256),
    )


def solution(mesh):
    return jax.shard_map(
        on_device,
        mesh=mesh,
        in_specs=(P("tm", "tile", None), P(), P(), P(), P(), P(), P(), P()),
        out_specs=P("tm", "tile", None, None, None),
        check_vma=False,
    )
```

time: 134 us -> 63.6 us (0.47)
  the two profiles are of different devices: /device:TPU:102 before, /device:TPU:1 now
where the time goes in v1:
time: 63.6 us; the launch traced here: 63.2 us
  local copies, waits for them, and re-layouts  23.9 us (38%)
  Pallas kernels  21.1 us (33%)
  starting transfers between devices  15.7 us (25%)
  waiting for transfers between devices  1.78 us (3%)
    pallas_call x1, Pallas kernels, on_device(): pl.pallas_call(section, out_shape=jax.ShapeDtypeStruct((3, 1, 2 * HL, 2 *...  18.5 us
    unnamed x18, local copies, waits for them, and re-layouts  18.4 us
    all_to_all x1, starting transfers between devices, exchange(): lax.all_to_all(send, ('tm', 'tile'), split_axis=0, concat_axis=0, tiled=T...  15.7 us
    pallas_call x1, Pallas kernels, on_device(): pl.pallas_call(prepare, out_shape=[pltpu.VMEM((9 * 128, 5 * C), bf16), pl...  2.68 us
    all_to_all x1, waiting for transfers between devices, exchange(): lax.all_to_all(send, ('tm', 'tile'), split_axis=0, concat_axis=0, tiled=T...  1.78 us
  transfers between devices with their start and end apart: 1, of which 1 were waited for; matrix products, arithmetic and copies ran while one was open for 4% of the time, Pallas kernels for 4%

profile of v1, /device:TPU:1, one launch (start us, length us, event | category | flops | bytes accessed | tf_op | source)
XLA Modules:
  0.0 63.2 jit_solution(531608837480919110)
XLA Ops:
  0.0 0.0 copy-start.1
  0.0 1.0 %reshape.77 = bf16[3,3,8,8,16]{4,3,2,1,0:T(8,128)(2,1)S(1)} reshape(bf16[3,3,1024]{2,1,0:T(4,128)(2,1)} %param.8) | data formatting | bytes 36864 | tf_op jit(solution)/shard_map/reshape | solution.py:19
  1.0 0.1 copy.14
  1.1 0.1 slice.44
  1.3 0.3 pad_maximum_fusion
  1.5 0.2 reshape.78
  1.7 0.2 concatenate.39
  2.0 0.1 fusion.7
  2.0 0.1 fusion.3
  2.2 0.1 maximum_bitcast_fusion
  2.3 0.1 copy.12
  2.4 1.0 %broadcast_in_dim.8 = bf16[4,64,2,384]{3,2,1,0:T(2,128)(2,1)} broadcast(bf16[64,2,384]{2,1,0:T(2,128)(2,1)S(1)} %copy.12), dimensions={1,2,3} | broadcast | bytes 491520 | tf_op jit(solution)/shard_map/broadcast_in_dim | solution.py:28
  3.3 15.7 %all-to-all-start = ((bf16[256,2,384]{2,1,0:T(2,128)(2,1)}), bf16[256,2,384]{2,1,0:T(2,128)(2,1)S(1)}, u32[]{:S(2)}, u32[]{:S(2)}) async-start(bf16[256,2,384]{2,1,0:T(2,128)(2,1)} %bitcast.8), calls=%async_computation | async-start | bytes 786432 | tf_op jit(solution)/shard_map/all_to_all | solution.py:29
  19.0 0.7 %reshape.84.b1_ref = f32[1,384]{1,0:T(1,128)S(1)} reshape(f32[384]{0:T(512)} %param.10) | data formatting | bytes 3072 | tf_op jit(solution)/shard_map/reshape | solution.py:215
  19.7 0.7 %reshape.85.gain_ref = f32[1,384]{1,0:T(1,128)S(1)} reshape(f32[384]{0:T(512)} %param.11) | data formatting | bytes 3072 | tf_op jit(solution)/shard_map/reshape | solution.py:216
  20.3 0.7 %reshape.86.b2_ref = f32[1,384]{1,0:T(1,128)S(1)} reshape(f32[384]{0:T(512)} %param.13) | data formatting | bytes 3072 | tf_op jit(solution)/shard_map/reshape | solution.py:217
  21.0 0.7 %pad.4 = f32[256]{0:T(256)S(1)} pad(f32[192]{0:T(256)} %param.15, f32[]{:T(128)} %constant.36.clone.1), padding=0_64 | pad | bytes 1796 | tf_op jit(solution)/shard_map/jit(_pad)/pad | solution.py:218
  21.7 0.0 copy-done.1
  21.7 3.3 %copy-done = bf16[3,3,3,384,384]{4,3,2,1,0:T(8,128)(2,1)S(1)} copy-done((bf16[3,3,3,384,384]{4,3,2,1,0:T(8,128)(2,1)S(1)}, bf16[3,3,3,384,384]{4,3,2,1,0:T(8,128)(2,1)}, u32[]{:S(2)}) %copy-start) | copy-done | bytes 7962648
  25.0 1.0 %copy-done.2 = bf16[3,3,3,16,384]{4,3,2,1,0:T(8,128)(2,1)S(1)} copy-done((bf16[3,3,3,16,384]{4,3,2,1,0:T(8,128)(2,1)S(1)}, bf16[3,3,3,16,384]{4,3,2,1,0:T(8,128)(2,1)}, u32[]{:S(2)}) %copy-start.2) | copy-done | bytes 331800
  26.0 2.7 %prepare.1 = (bf16[1152,1920]{1,0:T(8,128)(2,1)S(1)}, bf16[3456,1152]{1,0:T(8,128)(2,1)S(1)}, bf16[4,1536,256]{2,1,0:T(8,128)(2,1)S(1)}) custom-call(bf16[432,384]{1,0:T(8,128)(2,1)S(1)} %bitcast.25, bf16[3,3456,384]{2,1,0:T(8,128)(2,1)S(1)} %bitcast.23, bf16[9,192,384]{2,1,0:T(8,128)(2,1)S(1)} %bitcast.24), custom_call_target="tpu_custom_call" | custom-call | flops 1000000000 | bytes 20000000 | tf_op jit(solution)/shard_map/prepare/pallas_call | solution.py:176
  28.6 0.0 copy-start.3
  28.6 3.1 %copy-done.3 = bf16[3456,1152]{1,0:T(8,128)(2,1)} copy-done((bf16[3456,1152]{1,0:T(8,128)(2,1)}, bf16[3456,1152]{1,0:T(8,128)(2,1)S(1)}, u32[]{:S(2)}) %copy-start.3) | copy-done | bytes 7962648
  31.7 2.0 %copy-done.5 = bf16[1152,1920]{1,0:T(8,128)(2,1)} copy-done((bf16[1152,1920]{1,0:T(8,128)(2,1)}, bf16[1152,1920]{1,0:T(8,128)(2,1)S(1)}, u32[]{:S(2)}) %copy-start.5) | copy-done | bytes 4423704
  33.8 1.6 %copy-done.7 = bf16[4,1536,256]{2,1,0:T(8,128)(2,1)} copy-done((bf16[4,1536,256]{2,1,0:T(8,128)(2,1)}, bf16[4,1536,256]{2,1,0:T(8,128)(2,1)S(1)}, u32[]{:S(2)}) %copy-start.7) | copy-done | bytes 3145752
  35.4 1.8 %all-to-all-done = bf16[256,2,384]{2,1,0:T(2,128)(2,1)S(1)} async-done(((bf16[256,2,384]{2,1,0:T(2,128)(2,1)}), bf16[256,2,384]{2,1,0:T(2,128)(2,1)S(1)}, u32[]{:S(2)}, u32[]{:S(2)}) %all-to-all-start) | async-done | bytes 393248 | tf_op jit(solution)/shard_map/all_to_all | solution.py:29
  37.2 0.1 reshape.80.recv_ref
  37.3 0.0 copy-start.4
  37.3 3.3 %copy-done.4 = bf16[3456,1152]{1,0:T(8,128)(2,1)S(1)} copy-done((bf16[3456,1152]{1,0:T(8,128)(2,1)S(1)}, bf16[3456,1152]{1,0:T(8,128)(2,1)}, u32[]{:S(2)}) %copy-start.4) | copy-done | bytes 7962648
  40.6 2.3 %copy-done.6 = bf16[1152,1920]{1,0:T(8,128)(2,1)S(1)} copy-done((bf16[1152,1920]{1,0:T(8,128)(2,1)S(1)}, bf16[1152,1920]{1,0:T(8,128)(2,1)}, u32[]{:S(2)}) %copy-start.6) | copy-done | bytes 4423704
  42.8 1.9 %copy-done.8 = bf16[4,1536,256]{2,1,0:T(8,128)(2,1)S(1)} copy-done((bf16[4,1536,256]{2,1,0:T(8,128)(2,1)S(1)}, bf16[4,1536,256]{2,1,0:T(8,128)(2,1)}, u32[]{:S(2)}) %copy-start.8) | copy-done | bytes 3145752
  44.7 18.5 %section.1 = bf16[3,1,16,48,192]{4,3,2,1,0:T(8,128)(2,1)} custom-call(bf16[512,384]{1,0:T(8,128)(2,1)S(1)} %reshape.80.recv_ref, bf16[1152,1920]{1,0:T(8,128)(2,1)S(1)} %copy-done.6, bf16[3456,1152]{1,0:T(8,128)(2,1)S(1)} %copy-done.4, bf16[4,1536,256]{2,1,0:T(8,128)(2,1)S(1)} %copy-done.8, f32[1,384]{1,0:T(1,128)S(1)} %reshape.84.b1_ref, ...), custom_call_target="tpu_custom_call" | custom-call | flops 8000000000 | bytes 2000000 | tf_op jit(solution)/shard_map/section/pallas_call | solution.py:195
  (10 shorter events, 0.1 us)
Async XLA Ops:
  0.0 21.7 %copy-start.1 = (bf16[3,3,384,192]{2,3,1,0:T(8,128)(2,1)S(1)}, bf16[3,3,384,192]{2,3,1,0:T(8,128)(2,1)}, u32[]{:S(2)}) copy-start(bf16[3,3,384,192]{2,3,1,0:T(8,128)(2,1)} %param.14) | copy-start | bytes 3981316
  3.3 33.9 %all-to-all-start = ((bf16[256,2,384]{2,1,0:T(2,128)(2,1)}), bf16[256,2,384]{2,1,0:T(2,128)(2,1)S(1)}, u32[]{:S(2)}, u32[]{:S(2)}) async-start(bf16[256,2,384]{2,1,0:T(2,128)(2,1)} %bitcast.8), calls=%async_computation | async-start | bytes 786432 | tf_op jit(solution)/shard_map/all_to_all | solution.py:29
  21.7 3.3 %copy-start = (bf16[3,3,3,384,384]{4,3,2,1,0:T(8,128)(2,1)S(1)}, bf16[3,3,3,384,384]{4,3,2,1,0:T(8,128)(2,1)}, u32[]{:S(2)}) copy-start(bf16[3,3,3,384,384]{4,3,2,1,0:T(8,128)(2,1)} %param.12) | copy-start | bytes 23887876
  25.0 1.0 %copy-start.2 = (bf16[3,3,3,16,384]{4,3,2,1,0:T(8,128)(2,1)S(1)}, bf16[3,3,3,16,384]{4,3,2,1,0:T(8,128)(2,1)}, u32[]{:S(2)}) copy-start(bf16[3,3,3,16,384]{4,3,2,1,0:T(8,128)(2,1)} %param.9) | copy-start | bytes 995332
  28.6 3.1 %copy-start.3 = (bf16[3456,1152]{1,0:T(8,128)(2,1)}, bf16[3456,1152]{1,0:T(8,128)(2,1)S(1)}, u32[]{:S(2)}) copy-start(bf16[3456,1152]{1,0:T(8,128)(2,1)S(1)} %get-tuple-element.9.t2_ref) | copy-start | bytes 23887876
  31.7 2.0 %copy-start.5 = (bf16[1152,1920]{1,0:T(8,128)(2,1)}, bf16[1152,1920]{1,0:T(8,128)(2,1)S(1)}, u32[]{:S(2)}) copy-start(bf16[1152,1920]{1,0:T(8,128)(2,1)S(1)} %get-tuple-element.8.t1_ref) | copy-start | bytes 13271044
  33.8 1.6 %copy-start.7 = (bf16[4,1536,256]{2,1,0:T(8,128)(2,1)}, bf16[4,1536,256]{2,1,0:T(8,128)(2,1)S(1)}, u32[]{:S(2)}) copy-start(bf16[4,1536,256]{2,1,0:T(8,128)(2,1)S(1)} %get-tuple-element.10.tu_ref) | copy-start | bytes 9437188
  37.3 3.3 %copy-start.4 = (bf16[3456,1152]{1,0:T(8,128)(2,1)S(1)}, bf16[3456,1152]{1,0:T(8,128)(2,1)}, u32[]{:S(2)}) copy-start(bf16[3456,1152]{1,0:T(8,128)(2,1)} %copy-done.3) | copy-start | bytes 23887876
  40.6 2.3 %copy-start.6 = (bf16[1152,1920]{1,0:T(8,128)(2,1)S(1)}, bf16[1152,1920]{1,0:T(8,128)(2,1)}, u32[]{:S(2)}) copy-start(bf16[1152,1920]{1,0:T(8,128)(2,1)} %copy-done.5) | copy-start | bytes 13271044
  42.8 1.9 %copy-start.8 = (bf16[4,1536,256]{2,1,0:T(8,128)(2,1)S(1)}, bf16[4,1536,256]{2,1,0:T(8,128)(2,1)}, u32[]{:S(2)}) copy-start(bf16[4,1536,256]{2,1,0:T(8,128)(2,1)} %copy-done.7) | copy-start | bytes 9437188

commit v2 on v0

v2 whole, which is shorter than its diff:
```python
import jax
import jax.numpy as jnp
from jax import lax
from jax.experimental import pallas as pl
from jax.experimental.pallas import tpu as pltpu
from jax.sharding import PartitionSpec as P

LAT_C = 16
C = 384
C_UP = 192
HL = 8
WL = 24
GRID = 8
S = 32
M0, M1, M2, M3 = 14 * S, 12 * S, 10 * S, 8 * S
bf16, f32 = jnp.bfloat16, jnp.float32
VMEM = pl.BlockSpec(memory_space=pltpu.VMEM)
HBM = pl.BlockSpec(memory_space=pltpu.HBM)


def gather(latent):
    tiles = latent.reshape(3, 3, GRID, GRID, LAT_C).transpose(2, 3, 1, 0, 4)
    tiles = jnp.concatenate([tiles, tiles[:, :, :, 2:]], axis=3).reshape(GRID, GRID, 3 * 64)
    index = lax.axis_index("tile")
    r, g = index // GRID, index % GRID
    side = jnp.where(g < 4, jnp.roll(tiles, -1, axis=1), jnp.roll(tiles, 1, axis=1))
    wide = jnp.concatenate([tiles, side], axis=2)
    other = jnp.where(r < 4, jnp.roll(wide, -1, axis=0), jnp.roll(wide, 1, axis=0))
    pieces = jnp.stack([wide, other], axis=2).reshape(GRID * GRID, 2, 6 * 64)
    own = lax.all_to_all(pieces, "tile", split_axis=0, concat_axis=0, tiled=True)
    return own.reshape(GRID * GRID * 2, 6 * 64)


def place(shape, dim):
    return lax.broadcasted_iota(jnp.int32, shape, dim)


def origin():
    tile = lax.axis_index("tile")
    return lax.div(tile, GRID), lax.rem(tile, GRID)


def inside(rows, margin):
    a, b = origin()
    position = place((rows, 1), 0)
    row = (position >> 5) + a * HL - margin
    column = (position & 31) + b * WL - margin
    return (row >= 0) & (row < GRID * HL) & (column >= 0) & (column < GRID * WL)


def assemble(pieces_ref, own_ref, last_ref):
    a, b = origin()
    parts = []
    for j in range(3):
        group = pieces_ref[:, j * 128 : (j + 1) * 128].astype(f32)
        parts += [group, pltpu.roll(group, 64, 1)]
    stacked = jnp.concatenate(
        [parts[h * 3 + cell].astype(bf16) for cell in range(3) for h in range(2)], axis=0
    )
    row = place((M0, 1), 0)
    big_r, col = row >> 5, row & 31
    group = (col * 43) >> 7
    cell = col - 3 * group
    r = (big_r + 5) & 7
    g = (group + 7) & 7
    outer_r = jnp.where((big_r < 3) | (big_r >= 11), 1, 0)
    outer_g = jnp.where((group == 0) | (group == 9), 1, 0)
    source = cell * 256 + outer_g * 128 + r * 16 + g * 2 + outer_r
    source = jnp.where(inside(M0, 3) & (col < 30), source, -1)
    pick = jnp.where(place((M0, 768), 1) == source, 1.0, 0.0).astype(bf16)
    field = jnp.dot(pick, stacked, preferred_element_type=f32)
    half = M0 // 2
    lane = place((half, 128), 1)
    own_ref[...] = jnp.where(lane < 64, field[:half], pltpu.roll(field[half:], 64, 1)).astype(bf16)
    part = M0 // 8
    lane = place((part, 128), 1) >> 4
    last = jnp.zeros((part, 128), f32)
    for i in range(8):
        shift = (16 * i - 32) % 128
        rows = field[i * part : (i + 1) * part]
        last = jnp.where(lane == i, pltpu.roll(rows, shift, 1) if shift else rows, last)
    last_ref[...] = last.astype(bf16)


def side_by_side(x_ref, shift, target):
    low = place((M0, 128), 1) < 64
    left, middle, right = [
        pltpu.roll(x_ref[pl.ds(dx, M0), :], (64 * (dx % 2) + shift) % 128, 1) for dx in range(3)
    ]
    target[:, 0:128] = jnp.where(low, left, middle).astype(bf16)
    target[:, 128:256] = right.astype(bf16)


def taps(w1_ref, t1_ref, frames):
    t1_ref[...] = jnp.zeros(t1_ref.shape, t1_ref.dtype)
    for tap in range(9):
        for dt in range(3):
            for frame in range(frames):
                row = (tap // 3) * 256 + (tap % 3) * 64 + (frame + dt) * LAT_C
                source = (dt * 9 + tap) * LAT_C
                t1_ref[row : row + LAT_C, frame * C : (frame + 1) * C] = w1_ref[source : source + LAT_C, :]


def rows_of(ref, height):
    return jnp.concatenate([ref[dy * S : dy * S + height, :] for dy in range(3)], axis=1)


def spread(field_ref, height, target):
    for dx in range(3):
        target[:, dx * C : (dx + 1) * C] = field_ref[pl.ds(dx, height), :].astype(bf16)


def activate(start, gain, keep, act_ref, target):
    scaling = lax.rsqrt(jnp.mean(start * start, axis=1, keepdims=True) + 1e-06)
    value = start * scaling * gain
    value = value / (1.0 + jnp.exp(-value))
    act_ref[0:M1, :] = jnp.where(keep, value, 0.0)
    act_ref[M1 : M1 + 8, :] = jnp.zeros((8, C), f32)
    spread(act_ref, M1, target)


def front(
    own_ref, w1_ref, up_ref, w2_hbm, b1_ref, gain_ref, b2_ref, acc_ref, tu_ref, w2_ref,
    t1_ref, sem, x_ref, l1_ref, act_ref, la_ref,
):
    loads = [pltpu.make_async_copy(w2_hbm.at[dt], w2_ref.at[dt], sem.at[dt]) for dt in (2, 0, 1)]
    for load in loads:
        load.start()
    b1, gain, b2 = [ref[...].reshape(1, C) for ref in (b1_ref, gain_ref, b2_ref)]
    taps(w1_ref, t1_ref, 1)
    half = M0 // 2
    packed = own_ref[...].astype(f32)
    x_ref[0:half, :] = packed
    x_ref[half:M0, :] = pltpu.roll(packed, 64, 1)
    x_ref[M0 : M0 + 8, :] = jnp.zeros((8, 128), f32)
    side_by_side(x_ref, 0, l1_ref)
    field = jnp.dot(rows_of(l1_ref, M1), t1_ref[...], preferred_element_type=f32) + b1
    start = field.astype(bf16).astype(f32)
    act_ref[0:M1, :] = start
    residual = act_ref[pl.ds(S + 1, M2), :] + b2
    activate(start, gain, inside(M1, 2), act_ref, la_ref)
    groups = (((0,), (1, 2)), ((0, 1), (2,)))
    for py in range(2):
        for px in range(2):
            for ey in range(2):
                for ex in range(2):
                    total = None
                    for dy in groups[py][ey]:
                        for dx in groups[px][ex]:
                            part = up_ref[dy * 3 + dx].astype(f32)
                            total = part if total is None else total + part
                    row = (ey * 2 + ex) * C
                    tu_ref[py * 2 + px, row : row + C, 0:C_UP] = total.T.astype(bf16)
            tu_ref[py * 2 + px, :, C_UP:256] = jnp.zeros((4 * C, 256 - C_UP), bf16)
    loads[0].wait()
    acc_ref[...] = residual + jnp.dot(rows_of(la_ref, M2), w2_ref[2], preferred_element_type=f32)
    for load in loads[1:]:
        load.wait()


def back(
    own_ref, before_ref, older_ref, acc4_ref, w1_ref, tu_ref, w2_ref, b1_ref, gain_ref, b2_ref, bu_ref, out_hbm,
    t1_ref, sem, x_ref, l1_ref, act_ref, la_ref, acc_ref, lh_ref, up_ref, out_ref,
):
    b1, gain, b2 = [ref[...].reshape(1, C) for ref in (b1_ref, gain_ref, b2_ref)]
    bu = jnp.concatenate([bu_ref[...].reshape(1, C_UP), jnp.zeros((1, 256 - C_UP), f32)], axis=1)

    half, part = M0 // 2, M0 // 8
    now, before, older = [ref[...].astype(f32) for ref in (own_ref, before_ref, older_ref)]
    lane = place((half, 128), 1)
    for i in range(2):
        past = pltpu.roll(before, 64, 1) if i else before
        old = jnp.concatenate([pltpu.roll(older, 112 - 16 * (4 * i + k), 1) if 4 * i + k < 7 else older for k in range(4)], axis=0)
        x_ref[i * half : (i + 1) * half, :] = jnp.where(
            lane < 48, past, jnp.where(lane < 96, pltpu.roll(now, 112 if i else 48, 1), old)
        )
    x_ref[M0 : M0 + 8, :] = jnp.zeros((8, 128), f32)
    taps(w1_ref, t1_ref, 2)

    keep = inside(M1, 2)
    x = lax.axis_index("tm")
    for pair in range(2):
        side_by_side(x_ref, (16 - 32 * pair) % 128, l1_ref.at[pair])
        fields = jnp.dot(rows_of(l1_ref.at[pair], M1), t1_ref[...], preferred_element_type=f32)
        for k in range(2):
            frame = 2 * pair + k
            start = (fields[:, k * C : (k + 1) * C] + b1).astype(bf16).astype(f32)
            act = act_ref.at[frame]
            if pair:
                act[0:M1, :] = start
                acc_ref[:, k * C : (k + 1) * C] = act[pl.ds(S + 1, M2), :] + b2
            activate(start, gain, keep if pair else keep & (x > 0), act, la_ref.at[frame])
    acc_ref[:, 2 * C : 3 * C] = acc4_ref[...]

    for frame in range(4):
        low, high = max(0, frame - 2), min(2, frame)
        weight = jnp.concatenate([w2_ref[frame - t] for t in range(low, high + 1)], axis=1)
        acc_ref[:, low * C : (high + 1) * C] += jnp.dot(
            rows_of(la_ref.at[frame], M2), weight, preferred_element_type=f32
        )

    keep = inside(M2, 1)
    for t in range(3):
        act_ref[t, 0:M2, :] = jnp.where(keep, acc_ref[:, t * C : (t + 1) * C], 0.0)
        spread(act_ref.at[t], M2, lh_ref.at[t])
    for py in range(2):
        for px in range(2):
            lhs = jnp.concatenate(
                [
                    jnp.concatenate(
                        [
                            lh_ref[t, (py + ey) * S : (py + ey) * S + M3, (px + ex) * C : (px + ex + 1) * C]
                            for t in range(3)
                        ],
                        axis=0,
                    )
                    for ey in range(2)
                    for ex in range(2)
                ],
                axis=1,
            )
            phase = jnp.dot(lhs, tu_ref[py * 2 + px], preferred_element_type=f32) + bu
            for t in range(3):
                for y in range(HL):
                    row = t * M3 + y * S
                    for side in range(2):
                        up_ref[t, side, 2 * y + py, pl.ds(px, WL, stride=2), :] = phase[
                            row : row + WL, side * 128 : (side + 1) * 128
                        ]
    stores = []
    for t in range(3):
        out_ref[t, 0, :, :, 0:128] = up_ref[t, 0].astype(bf16)
        out_ref[t, 0, :, :, 128:C_UP] = up_ref[t, 1, :, :, 0 : C_UP - 128].astype(bf16)
        stores.append(pltpu.make_async_copy(out_ref.at[t], out_hbm.at[t], sem.at[t]))
        stores[-1].start()
    for store in stores:
        store.wait()


def on_device(
    latent, conv_in_weight, conv_in_bias, first_gain, conv_weight, conv_bias, up_weight, up_bias
):
    w1 = conv_in_weight.reshape(27 * LAT_C, C)
    w2 = pltpu.with_memory_space_constraint(conv_weight.reshape(3, 9 * C, C), pltpu.HBM)
    own, last = pl.pallas_call(
        assemble,
        out_shape=[jax.ShapeDtypeStruct((M0 // 2, 128), bf16), jax.ShapeDtypeStruct((M0 // 8, 128), bf16)],
        in_specs=[VMEM],
        out_specs=[VMEM, VMEM],
        compiler_params=pltpu.CompilerParams(vmem_limit_bytes=8 * 2**20),
        cost_estimate=pl.CostEstimate(flops=10**8, bytes_accessed=10**6, transcendentals=0),
        name="assemble",
    )(gather(latent))
    count = lax.axis_size("tm")
    before = lax.ppermute(own, "tm", [(i, i + 1) for i in range(count - 1)])
    older = lax.ppermute(last, "tm", [(i, i + 2) for i in range(count - 2)])
    acc4, tu, w2 = pl.pallas_call(
        front,
        out_shape=[
            jax.ShapeDtypeStruct((M2, C), f32),
            jax.ShapeDtypeStruct((4, 4 * C, 256), bf16),
            pltpu.VMEM((3, 9 * C, C), bf16),
        ],
        in_specs=[VMEM, VMEM, VMEM, HBM, VMEM, VMEM, VMEM],
        out_specs=[VMEM, VMEM, VMEM],
        scratch_shapes=[
            pltpu.VMEM((3 * 256, C), bf16),
            pltpu.SemaphoreType.DMA((3,)),
            pltpu.VMEM((M0 + 8, 128), f32),
            pltpu.VMEM((M0, 256), bf16),
            pltpu.VMEM((M1 + 8, C), f32),
            pltpu.VMEM((M1, 3 * C), bf16),
        ],
        compiler_params=pltpu.CompilerParams(vmem_limit_bytes=24 * 2**20),
        cost_estimate=pl.CostEstimate(flops=10**9, bytes_accessed=10_000_000, transcendentals=10**6),
        name="front",
    )(own, w1, up_weight.transpose(0, 1, 3, 2).reshape(9, C_UP, C), w2, conv_in_bias, first_gain, conv_bias)
    return pl.pallas_call(
        back,
        out_shape=jax.ShapeDtypeStruct((3, 1, 2 * HL, 2 * WL, C_UP), bf16),
        in_specs=[VMEM] * 11,
        out_specs=HBM,
        scratch_shapes=[
            pltpu.VMEM((3 * 256, 2 * C), bf16),
            pltpu.SemaphoreType.DMA((3,)),
            pltpu.VMEM((M0 + 8, 128), f32),
            pltpu.VMEM((2, M0, 256), bf16),
            pltpu.VMEM((4, M1 + 8, C), f32),
            pltpu.VMEM((4, M1, 3 * C), bf16),
            pltpu.VMEM((M2, 3 * C), f32),
            pltpu.VMEM((3, M2, 3 * C), bf16),
            pltpu.VMEM((3, 2, 2 * HL, 2 * WL, 128), f32),
            pltpu.VMEM((3, 1, 2 * HL, 2 * WL, C_UP), bf16),
        ],
        compiler_params=pltpu.CompilerParams(vmem_limit_bytes=32 * 2**20),
        cost_estimate=pl.CostEstimate(flops=8 * 10**9, bytes_accessed=12_000_000, transcendentals=10**6),
        name="back",
    )(own, before, older, acc4, w1, tu, w2, conv_in_bias, first_gain, conv_bias, up_bias)


def solution(mesh):
    return jax.shard_map(
        on_device,
        mesh=mesh,
        in_specs=(P("tm", "tile", None), P(), P(), P(), P(), P(), P(), P()),
        out_specs=P("tm", "tile", None, None, None),
        check_vma=False,
    )
```

time: 134 us -> 52.9 us (0.39)
  the two profiles are of different devices: /device:TPU:102 before, /device:TPU:1 now
where the time goes in v2:
time: 52.9 us; the launch traced here: 52.7 us
  blocking collectives  23.5 us (44%)
  Pallas kernels  19.4 us (37%)
  starting transfers between devices  7.05 us (13%)
  local copies, waits for them, and re-layouts  1.77 us (3%)
  other arithmetic  0.57 us (1%)
    all_to_all x1, blocking collectives, gather(): lax.all_to_all(pieces, 'tile', split_axis=0, concat_axis=0, tiled=True)  23.5 us
    pallas_call x1, Pallas kernels, on_device(): pl.pallas_call(back, out_shape=jax.ShapeDtypeStruct((3, 1, 2 * HL, 2 * WL...  14.8 us
    ppermute x1, starting transfers between devices, on_device(): older = lax.ppermute(last, 'tm', [(i, i + 2) for i in range(count - 2)])  4.65 us
    pallas_call x1, Pallas kernels, on_device(): pl.pallas_call(front, out_shape=[jax.ShapeDtypeStruct((M2, C), f32), jax....  3.95 us
    ppermute x1, starting transfers between devices, on_device(): before = lax.ppermute(own, 'tm', [(i, i + 1) for i in range(count - 1)])  2.4 us
    reshape x2, local copies, waits for them, and re-layouts, gather(): tiles = latent.reshape(3, 3, GRID, GRID, LAT_C).transpose(2, 3, 1, 0, 4)  1.14 us
  transfers between devices with their start and end apart: 2, of which 0 were waited for; matrix products, arithmetic and copies ran while one was open for 0% of the time, Pallas kernels for 7%

profile of v2, /device:TPU:1, one launch (start us, length us, event | category | flops | bytes accessed | tf_op | source)
XLA Modules:
  0.0 52.7 jit_solution(14852384227379341270)
XLA Ops:
  0.0 0.0 copy-start.4
  0.0 0.0 copy-start.3
  0.0 0.0 copy-start.2
  0.0 0.0 copy-start
  0.0 0.0 copy-start.1
  0.0 1.0 %reshape.62 = bf16[3,3,8,8,16]{4,3,2,1,0:T(8,128)(2,1)S(1)} reshape(bf16[3,3,1024]{2,1,0:T(4,128)(2,1)} %param.8) | data formatting | bytes 36864 | tf_op jit(solution)/shard_map/reshape | solution.py:22
  1.1 0.1 copy.17
  1.2 0.1 slice.44
  1.3 0.3 pad_maximum_fusion
  1.6 0.2 reshape.63
  1.8 0.2 concatenate.39
  2.0 0.1 fusion.7
  2.1 0.1 fusion.3
  2.2 0.1 pad_maximum_fusion.1
  2.3 0.1 copy.15
  2.4 23.5 %all_to_all.5 = bf16[64,2,384]{2,1,0:T(2,128)(2,1)S(1)} all-to-all(bf16[64,2,384]{2,1,0:T(2,128)(2,1)S(1)} %copy.15), channel_id=1, replica_groups=mesh['tile'=64,'tm'=4] {'tile'}, dimensions={0} | all-to-all | bytes 196608 | tf_op jit(solution)/shard_map/all_to_all | solution.py:30
  26.0 0.6 %assemble.1 = (bf16[224,128]{1,0:T(8,128)(2,1)S(1)}, bf16[56,128]{1,0:T(8,128)(2,1)S(1)}) custom-call(bf16[128,384]{1,0:T(8,128)(2,1)S(1)} %reshape.64.pieces_ref), custom_call_target="tpu_custom_call" | custom-call | flops 100000000 | bytes 1000000 | tf_op jit(solution)/shard_map/assemble/pallas_call | solution.py:245
  26.6 4.6 %collective-permute-start.1 = (bf16[56,128]{1,0:T(8,128)(2,1)S(1)}, bf16[56,128]{1,0:T(8,128)(2,1)S(1)}, u32[]{:S(2)}, u32[]{:S(2)}) collective-permute-start(bf16[56,128]{1,0:T(8,128)(2,1)S(1)} %get-tuple-element.11), channel_id=1, source_target_pairs={{0,2},{1,3},{4,6},{5,7},{8,10},{9,11},{12,14},{13,15},{16,18},{17,... | collective-permute-start | bytes 43016 | tf_op jit(solution)/shard_map/ppermute | solution.py:256
  31.3 2.4 %collective-permute-start = (bf16[224,128]{1,0:T(8,128)(2,1)S(1)}, bf16[224,128]{1,0:T(8,128)(2,1)S(1)}, u32[]{:S(2)}, u32[]{:S(2)}) collective-permute-start(bf16[224,128]{1,0:T(8,128)(2,1)S(1)} %get-tuple-element.10.own_ref), channel_id=1, source_target_pairs={{0,1},{1,2},{2,3},{4,5},{5,6},{6,7},{8,9},{9,10},{10,11},{12,13},{... | collective-permute-start | bytes 172040 | tf_op jit(solution)/shard_map/ppermute | solution.py:255
  33.7 0.0 copy-done.4
  33.7 0.0 copy-done.3
  33.7 0.0 copy-done.2
  33.7 0.0 copy-done
  33.7 0.0 copy-done.1
  33.7 0.0 copy-start.5
  33.8 3.9 %front.1 = (f32[320,384]{1,0:T(8,128)S(1)}, bf16[4,1536,256]{2,1,0:T(8,128)(2,1)S(1)}, bf16[3,3456,384]{2,1,0:T(8,128)(2,1)S(1)}) custom-call(bf16[224,128]{1,0:T(8,128)(2,1)S(1)} %get-tuple-element.10.own_ref, bf16[432,384]{1,0:T(8,128)(2,1)S(1)} %bitcast.20, bf16[9,192,384]{2,1,0:T(8,128)(2,1)S(1)} %bitcast.19, bf16[3,3456,384]{2,1,0:T(8,128)(2,1)} %bitcast.22, ...), custom_call_target="tpu_custom_call" | custom-call | flops 1000000000 | bytes 10000000 | tf_op jit(solution)/shard_map/front/pallas_call | solution.py:257
  37.7 0.0 collective-permute-done.1.older_ref
  37.7 0.0 collective-permute-done.before_ref
  37.7 0.0 copy-done.5
  37.7 14.8 %back.1 = bf16[3,1,16,48,192]{4,3,2,1,0:T(8,128)(2,1)} custom-call(bf16[224,128]{1,0:T(8,128)(2,1)S(1)} %get-tuple-element.10.own_ref, bf16[224,128]{1,0:T(8,128)(2,1)S(1)} %collective-permute-done.before_ref, bf16[56,128]{1,0:T(8,128)(2,1)S(1)} %collective-permute-done.1.older_ref, f32[320,384]{1,0:T(8,128)S(1)} %get-tuple-element.12.acc4_ref, ...), custom_call_target="tpu_custom_call" | custom-call | flops 8000000000 | bytes 12000000 | tf_op jit(solution)/shard_map/back/pallas_call | solution.py:278
  (5 shorter events, 0.1 us)
Async XLA Ops:
  0.0 33.7 %copy-start.4 = (f32[384]{0:T(512)S(1)}, f32[384]{0:T(512)}, u32[]{:S(2)}) copy-start(f32[384]{0:T(512)} %b2_ref.3) | copy-start | bytes 4612
  0.0 33.7 %copy-start.3 = (f32[384]{0:T(512)S(1)}, f32[384]{0:T(512)}, u32[]{:S(2)}) copy-start(f32[384]{0:T(512)} %gain_ref.3) | copy-start | bytes 4612
  0.0 33.7 %copy-start.2 = (f32[384]{0:T(512)S(1)}, f32[384]{0:T(512)}, u32[]{:S(2)}) copy-start(f32[384]{0:T(512)} %b1_ref.3) | copy-start | bytes 4612
  0.0 33.7 %copy-start = (bf16[3,3,384,192]{2,3,1,0:T(8,128)(2,1)S(1)}, bf16[3,3,384,192]{2,3,1,0:T(8,128)(2,1)}, u32[]{:S(2)}) copy-start(bf16[3,3,384,192]{2,3,1,0:T(8,128)(2,1)} %param.14) | copy-start | bytes 3981316
  0.0 33.7 %copy-start.1 = (bf16[3,3,3,16,384]{4,3,2,1,0:T(8,128)(2,1)S(1)}, bf16[3,3,3,16,384]{4,3,2,1,0:T(8,128)(2,1)}, u32[]{:S(2)}) copy-start(bf16[3,3,3,16,384]{4,3,2,1,0:T(8,128)(2,1)} %param.9) | copy-start | bytes 995332
  26.6 11.1 %collective-permute-start.1 = (bf16[56,128]{1,0:T(8,128)(2,1)S(1)}, bf16[56,128]{1,0:T(8,128)(2,1)S(1)}, u32[]{:S(2)}, u32[]{:S(2)}) collective-permute-start(bf16[56,128]{1,0:T(8,128)(2,1)S(1)} %get-tuple-element.11), channel_id=1, source_target_pairs={{0,2},{1,3},{4,6},{5,7},{8,10},{9,11},{12,14},{13,15},{16,18},{17,... | collective-permute-start | bytes 43016 | tf_op jit(solution)/shard_map/ppermute | solution.py:256
  31.3 6.4 %collective-permute-start = (bf16[224,128]{1,0:T(8,128)(2,1)S(1)}, bf16[224,128]{1,0:T(8,128)(2,1)S(1)}, u32[]{:S(2)}, u32[]{:S(2)}) collective-permute-start(bf16[224,128]{1,0:T(8,128)(2,1)S(1)} %get-tuple-element.10.own_ref), channel_id=1, source_target_pairs={{0,1},{1,2},{2,3},{4,5},{5,6},{6,7},{8,9},{9,10},{10,11},{12,13},{... | collective-permute-start | bytes 172040 | tf_op jit(solution)/shard_map/ppermute | solution.py:255
  33.7 4.0 %copy-start.5 = (f32[192]{0:T(256)S(1)}, f32[192]{0:T(256)}, u32[]{:S(2)}) copy-start(f32[192]{0:T(256)} %bu_ref.1) | copy-start | bytes 2308

commit v3 on v2

--- a/solution.py
+++ b/solution.py
@@ -166,7 +166,10 @@
     bu = jnp.concatenate([bu_ref[...].reshape(1, C_UP), jnp.zeros((1, 256 - C_UP), f32)], axis=1)
 
     half, part = M0 // 2, M0 // 8
-    now, before, older = [ref[...].astype(f32) for ref in (own_ref, before_ref, older_ref)]
+    x = lax.axis_index("tm")
+    now, before, older = [
+        jnp.where(x >= d, ref[...].astype(f32), 0.0) for d, ref in enumerate((own_ref, before_ref, older_ref))
+    ]
     lane = place((half, 128), 1)
     for i in range(2):
         past = pltpu.roll(before, 64, 1) if i else before
@@ -178,7 +181,6 @@
     taps(w1_ref, t1_ref, 2)
 
     keep = inside(M1, 2)
-    x = lax.axis_index("tm")
     for pair in range(2):
         side_by_side(x_ref, (16 - 32 * pair) % 128, l1_ref.at[pair])
         fields = jnp.dot(rows_of(l1_ref.at[pair], M1), t1_ref[...], preferred_element_type=f32)
@@ -252,8 +254,8 @@
         name="assemble",
     )(gather(latent))
     count = lax.axis_size("tm")
-    before = lax.ppermute(own, "tm", [(i, i + 1) for i in range(count - 1)])
-    older = lax.ppermute(last, "tm", [(i, i + 2) for i in range(count - 2)])
+    before = lax.ppermute(own, "tm", [(i, (i + 1) % count) for i in range(count)])
+    older = lax.ppermute(last, "tm", [(i, (i + 2) % count) for i in range(count)])
     acc4, tu, w2 = pl.pallas_call(
         front,
         out_shape=[

time: 52.9 us -> 48.9 us (0.924)
  starting transfers between devices: 7.05 us -> 3.14 us
    ppermute x2, starting transfers between devices: 7.05 us -> 3.14 us  [the longest x1 2.83 us: on_device(): lax.ppermute(last, 'tm', [(i, (i + 2) % count) for i in range(count)])]
  transfers between devices with their start and end apart: 2 -> 2, of which waited for: 0 -> 0; matrix products, arithmetic and copies ran while one was open for 0% -> 0% of each run, Pallas kernels for 7% -> 8%
where the time goes in v3:
time: 48.9 us; the launch traced here: 48.8 us
  blocking collectives  23.5 us (48%)
  Pallas kernels  19.4 us (40%)
  starting transfers between devices  3.14 us (6%)
  local copies, waits for them, and re-layouts  1.77 us (4%)
  other arithmetic  0.57 us (1%)
    all_to_all x1, blocking collectives, gather(): lax.all_to_all(pieces, 'tile', split_axis=0, concat_axis=0, tiled=True)  23.5 us
    pallas_call x1, Pallas kernels, on_device(): pl.pallas_call(back, out_shape=jax.ShapeDtypeStruct((3, 1, 2 * HL, 2 * WL...  14.8 us
    pallas_call x1, Pallas kernels, on_device(): pl.pallas_call(front, out_shape=[jax.ShapeDtypeStruct((M2, C), f32), jax....  3.95 us
    ppermute x1, starting transfers between devices, on_device(): lax.ppermute(last, 'tm', [(i, (i + 2) % count) for i in range(count)])  2.83 us
    reshape x2, local copies, waits for them, and re-layouts, gather(): tiles = latent.reshape(3, 3, GRID, GRID, LAT_C).transpose(2, 3, 1, 0, 4)  1.14 us
  transfers between devices with their start and end apart: 2, of which 0 were waited for; matrix products, arithmetic and copies ran while one was open for 0% of the time, Pallas kernels for 8%

profile of v3, /device:TPU:1, one launch (start us, length us, event | category | flops | bytes accessed | tf_op | source)
XLA Modules:
  0.0 48.8 jit_solution(11597634738152492070)
XLA Ops:
  0.0 0.0 copy-start.4
  0.0 0.0 copy-start.3
  0.0 0.0 copy-start.2
  0.0 0.0 copy-start
  0.0 0.0 copy-start.1
  0.0 1.0 %reshape.62 = bf16[3,3,8,8,16]{4,3,2,1,0:T(8,128)(2,1)S(1)} reshape(bf16[3,3,1024]{2,1,0:T(4,128)(2,1)} %param.8) | data formatting | bytes 36864 | tf_op jit(solution)/shard_map/reshape | solution.py:22
  1.1 0.1 copy.17
  1.2 0.1 slice.44
  1.3 0.3 pad_maximum_fusion
  1.6 0.2 reshape.63
  1.8 0.2 concatenate.39
  2.0 0.1 fusion.7
  2.1 0.1 fusion.3
  2.2 0.1 pad_maximum_fusion.1
  2.3 0.1 copy.15
  2.4 23.5 %all_to_all.5 = bf16[64,2,384]{2,1,0:T(2,128)(2,1)S(1)} all-to-all(bf16[64,2,384]{2,1,0:T(2,128)(2,1)S(1)} %copy.15), channel_id=1, replica_groups=mesh['tile'=64,'tm'=4] {'tile'}, dimensions={0} | all-to-all | bytes 196608 | tf_op jit(solution)/shard_map/all_to_all | solution.py:30
  26.0 0.6 %assemble.1 = (bf16[224,128]{1,0:T(8,128)(2,1)S(1)}, bf16[56,128]{1,0:T(8,128)(2,1)S(1)}) custom-call(bf16[128,384]{1,0:T(8,128)(2,1)S(1)} %reshape.64.pieces_ref), custom_call_target="tpu_custom_call" | custom-call | flops 100000000 | bytes 1000000 | tf_op jit(solution)/shard_map/assemble/pallas_call | solution.py:247
  26.6 2.8 %collective-permute-start.1 = (bf16[56,128]{1,0:T(8,128)(2,1)S(1)}, bf16[56,128]{1,0:T(8,128)(2,1)S(1)}, u32[]{:S(2)}, u32[]{:S(2)}) collective-permute-start(bf16[56,128]{1,0:T(8,128)(2,1)S(1)} %get-tuple-element.11), channel_id=1, source_target_pairs={{0,2},{1,3},{2,0},{3,1},{4,6},{5,7},{6,4},{7,5},{8,10},{9,11},{10,... | collective-permute-start | bytes 43016 | tf_op jit(solution)/shard_map/ppermute | solution.py:258
  29.5 0.3 collective-permute-start
  29.8 0.0 copy-done.4
  29.8 0.0 copy-done.3
  29.8 0.0 copy-done.2
  29.8 0.0 copy-done
  29.8 0.0 copy-done.1
  29.8 0.0 copy-start.5
  29.8 3.9 %front.1 = (f32[320,384]{1,0:T(8,128)S(1)}, bf16[4,1536,256]{2,1,0:T(8,128)(2,1)S(1)}, bf16[3,3456,384]{2,1,0:T(8,128)(2,1)S(1)}) custom-call(bf16[224,128]{1,0:T(8,128)(2,1)S(1)} %get-tuple-element.10.own_ref, bf16[432,384]{1,0:T(8,128)(2,1)S(1)} %bitcast.20, bf16[9,192,384]{2,1,0:T(8,128)(2,1)S(1)} %bitcast.19, bf16[3,3456,384]{2,1,0:T(8,128)(2,1)} %bitcast.22, ...), custom_call_target="tpu_custom_call" | custom-call | flops 1000000000 | bytes 10000000 | tf_op jit(solution)/shard_map/front/pallas_call | solution.py:259
  33.8 0.0 collective-permute-done.1.older_ref
  33.8 0.0 collective-permute-done.before_ref
  33.8 0.0 copy-done.5
  33.8 14.8 %back.1 = bf16[3,1,16,48,192]{4,3,2,1,0:T(8,128)(2,1)} custom-call(bf16[224,128]{1,0:T(8,128)(2,1)S(1)} %get-tuple-element.10.own_ref, bf16[224,128]{1,0:T(8,128)(2,1)S(1)} %collective-permute-done.before_ref, bf16[56,128]{1,0:T(8,128)(2,1)S(1)} %collective-permute-done.1.older_ref, f32[320,384]{1,0:T(8,128)S(1)} %get-tuple-element.12.acc4_ref, ...), custom_call_target="tpu_custom_call" | custom-call | flops 8000000000 | bytes 12000000 | tf_op jit(solution)/shard_map/back/pallas_call | solution.py:280
  (5 shorter events, 0.1 us)
Async XLA Ops:
  0.0 29.8 %copy-start.4 = (f32[384]{0:T(512)S(1)}, f32[384]{0:T(512)}, u32[]{:S(2)}) copy-start(f32[384]{0:T(512)} %b2_ref.3) | copy-start | bytes 4612
  0.0 29.8 %copy-start.3 = (f32[384]{0:T(512)S(1)}, f32[384]{0:T(512)}, u32[]{:S(2)}) copy-start(f32[384]{0:T(512)} %gain_ref.3) | copy-start | bytes 4612
  0.0 29.8 %copy-start.2 = (f32[384]{0:T(512)S(1)}, f32[384]{0:T(512)}, u32[]{:S(2)}) copy-start(f32[384]{0:T(512)} %b1_ref.3) | copy-start | bytes 4612
  0.0 29.8 %copy-start = (bf16[3,3,384,192]{2,3,1,0:T(8,128)(2,1)S(1)}, bf16[3,3,384,192]{2,3,1,0:T(8,128)(2,1)}, u32[]{:S(2)}) copy-start(bf16[3,3,384,192]{2,3,1,0:T(8,128)(2,1)} %param.14) | copy-start | bytes 3981316
  0.0 29.8 %copy-start.1 = (bf16[3,3,3,16,384]{4,3,2,1,0:T(8,128)(2,1)S(1)}, bf16[3,3,3,16,384]{4,3,2,1,0:T(8,128)(2,1)}, u32[]{:S(2)}) copy-start(bf16[3,3,3,16,384]{4,3,2,1,0:T(8,128)(2,1)} %param.9) | copy-start | bytes 995332
  26.6 7.1 %collective-permute-start.1 = (bf16[56,128]{1,0:T(8,128)(2,1)S(1)}, bf16[56,128]{1,0:T(8,128)(2,1)S(1)}, u32[]{:S(2)}, u32[]{:S(2)}) collective-permute-start(bf16[56,128]{1,0:T(8,128)(2,1)S(1)} %get-tuple-element.11), channel_id=1, source_target_pairs={{0,2},{1,3},{2,0},{3,1},{4,6},{5,7},{6,4},{7,5},{8,10},{9,11},{10,... | collective-permute-start | bytes 43016 | tf_op jit(solution)/shard_map/ppermute | solution.py:258
  29.5 4.3 %collective-permute-start = (bf16[224,128]{1,0:T(8,128)(2,1)S(1)}, bf16[224,128]{1,0:T(8,128)(2,1)S(1)}, u32[]{:S(2)}, u32[]{:S(2)}) collective-permute-start(bf16[224,128]{1,0:T(8,128)(2,1)S(1)} %get-tuple-element.10.own_ref), channel_id=1, source_target_pairs={{0,1},{1,2},{2,3},{3,0},{4,5},{5,6},{6,7},{7,4},{8,9},{9,10},{10,1... | collective-permute-start | bytes 172040 | tf_op jit(solution)/shard_map/ppermute | solution.py:257
  29.8 4.0 %copy-start.5 = (f32[192]{0:T(256)S(1)}, f32[192]{0:T(256)}, u32[]{:S(2)}) copy-start(f32[192]{0:T(256)} %bu_ref.1) | copy-start | bytes 2308

commit v4 on v3

--- a/solution.py
+++ b/solution.py
@@ -12,7 +12,9 @@
 WL = 24
 GRID = 8
 S = 32
-M0, M1, M2, M3 = 14 * S, 12 * S, 10 * S, 8 * S
+M0, M1 = 14 * S, 12 * S
+EDGES = 24
+CORE, M2, M3 = 10 * WL, 10 * WL + EDGES, HL * WL
 bf16, f32 = jnp.bfloat16, jnp.float32
 VMEM = pl.BlockSpec(memory_space=pltpu.VMEM)
 HBM = pl.BlockSpec(memory_space=pltpu.HBM)
@@ -105,18 +107,48 @@
     return jnp.concatenate([ref[dy * S : dy * S + height, :] for dy in range(3)], axis=1)
 
 
-def spread(field_ref, height, target):
-    for dx in range(3):
-        target[:, dx * C : (dx + 1) * C] = field_ref[pl.ds(dx, height), :].astype(bf16)
-
-
-def activate(start, gain, keep, act_ref, target):
+def lanes(l, first=0):
+    return slice(first + l * 128, first + (l + 1) * 128)
+
+
+def strip(ref, l, first, height):
+    return jnp.concatenate([ref[l, pl.ds(first + y * S, WL), :] for y in range(height)], axis=0)
+
+
+def edge(ref, l, first, rim_ref):
+    for s in range(2):
+        rim_ref[pl.ds(s, 10, stride=2), :] = ref[l, pl.ds(first + 25 * s, 10, stride=S), :]
+    return rim_ref[...]
+
+
+def silu_of_norm(start, gain):
     scaling = lax.rsqrt(jnp.mean(start * start, axis=1, keepdims=True) + 1e-06)
     value = start * scaling * gain
-    value = value / (1.0 + jnp.exp(-value))
-    act_ref[0:M1, :] = jnp.where(keep, value, 0.0)
-    act_ref[M1 : M1 + 8, :] = jnp.zeros((8, C), f32)
-    spread(act_ref, M1, target)
+    return value / (1.0 + jnp.exp(-value))
+
+
+def residual(start, b2, act_ref, rim_ref, target, first):
+    for l in range(3):
+        act_ref[l] = start[:, lanes(l)]
+        target[0:CORE, lanes(l, first)] = strip(act_ref, l, S + 2, 10) + b2[:, lanes(l)]
+        target[CORE:M2, lanes(l, first)] = edge(act_ref, l, S + 1, rim_ref.at[27 + l]) + b2[:, lanes(l)]
+
+
+def activate(start, gain, keep, act_ref, rim_ref, la_ref, le_ref):
+    value = jnp.where(keep, silu_of_norm(start, gain), 0.0)
+    for l in range(3):
+        act_ref[l] = value[:, lanes(l)]
+        for dx in range(3):
+            for y in range(0, 12, 2):
+                la_ref[y * WL : (y + 2) * WL, lanes(l, dx * C)] = strip(act_ref, l, y * S + 1 + dx, 2).astype(bf16)
+            for dy in range(3):
+                rim = edge(act_ref, l, dy * S + dx, rim_ref.at[(dy * 3 + dx) * 3 + l])
+                le_ref[:, lanes(l, (dy * 3 + dx) * C)] = rim.astype(bf16)
+
+
+def taps_of(la_ref, le_ref):
+    core = jnp.concatenate([la_ref[dy * WL : dy * WL + CORE, :] for dy in range(3)], axis=1)
+    return jnp.concatenate([core, le_ref[...]], axis=0)
 
 
 def front(
@@ -137,8 +169,11 @@
     field = jnp.dot(rows_of(l1_ref, M1), t1_ref[...], preferred_element_type=f32) + b1
     start = field.astype(bf16).astype(f32)
     act_ref[0:M1, :] = start
-    residual = act_ref[pl.ds(S + 1, M2), :] + b2
-    activate(start, gain, inside(M1, 2), act_ref, la_ref)
+    kept = act_ref[pl.ds(S + 1, 10 * S), :] + b2
+    act_ref[0:M1, :] = jnp.where(inside(M1, 2), silu_of_norm(start, gain), 0.0)
+    act_ref[M1 : M1 + 8, :] = jnp.zeros((8, C), f32)
+    for dx in range(3):
+        la_ref[:, dx * C : (dx + 1) * C] = act_ref[pl.ds(dx, M1), :].astype(bf16)
     groups = (((0,), (1, 2)), ((0, 1), (2,)))
     for py in range(2):
         for px in range(2):
@@ -153,14 +188,16 @@
                     tu_ref[py * 2 + px, row : row + C, 0:C_UP] = total.T.astype(bf16)
             tu_ref[py * 2 + px, :, C_UP:256] = jnp.zeros((4 * C, 256 - C_UP), bf16)
     loads[0].wait()
-    acc_ref[...] = residual + jnp.dot(rows_of(la_ref, M2), w2_ref[2], preferred_element_type=f32)
+    field = kept + jnp.dot(rows_of(la_ref, 10 * S), w2_ref[2], preferred_element_type=f32)
+    for l in range(3):
+        acc_ref[l] = field[:, lanes(l)]
     for load in loads[1:]:
         load.wait()
 
 
 def back(
     own_ref, before_ref, older_ref, acc4_ref, w1_ref, tu_ref, w2_ref, b1_ref, gain_ref, b2_ref, bu_ref, out_hbm,
-    t1_ref, sem, x_ref, l1_ref, act_ref, la_ref, acc_ref, lh_ref, up_ref, out_ref,
+    t1_ref, sem, x_ref, l1_ref, act_ref, rim_ref, la_ref, le_ref, acc_ref, lh_ref, up_ref, out_ref,
 ):
     b1, gain, b2 = [ref[...].reshape(1, C) for ref in (b1_ref, gain_ref, b2_ref)]
     bu = jnp.concatenate([bu_ref[...].reshape(1, C_UP), jnp.zeros((1, 256 - C_UP), f32)], axis=1)
@@ -180,6 +217,7 @@
     x_ref[M0 : M0 + 8, :] = jnp.zeros((8, 128), f32)
     taps(w1_ref, t1_ref, 2)
 
+    rim_ref[...] = jnp.zeros(rim_ref.shape, f32)
     keep = inside(M1, 2)
     for pair in range(2):
         side_by_side(x_ref, (16 - 32 * pair) % 128, l1_ref.at[pair])
@@ -187,31 +225,48 @@
         for k in range(2):
             frame = 2 * pair + k
             start = (fields[:, k * C : (k + 1) * C] + b1).astype(bf16).astype(f32)
-            act = act_ref.at[frame]
             if pair:
-                act[0:M1, :] = start
-                acc_ref[:, k * C : (k + 1) * C] = act[pl.ds(S + 1, M2), :] + b2
-            activate(start, gain, keep if pair else keep & (x > 0), act, la_ref.at[frame])
-    acc_ref[:, 2 * C : 3 * C] = acc4_ref[...]
+                residual(start, b2, act_ref.at[frame], rim_ref.at[frame], acc_ref, k * C)
+            activate(
+                start, gain, keep if pair else keep & (x > 0), act_ref.at[frame], rim_ref.at[frame],
+                la_ref.at[frame], le_ref.at[frame],
+            )
+    for l in range(3):
+        acc_ref[0:CORE, lanes(l, 2 * C)] = strip(acc4_ref, l, 1, 10)
+        acc_ref[CORE:M2, lanes(l, 2 * C)] = edge(acc4_ref, l, 0, rim_ref.at[0, 27 + l])
 
     for frame in range(4):
         low, high = max(0, frame - 2), min(2, frame)
         weight = jnp.concatenate([w2_ref[frame - t] for t in range(low, high + 1)], axis=1)
         acc_ref[:, low * C : (high + 1) * C] += jnp.dot(
-            rows_of(la_ref.at[frame], M2), weight, preferred_element_type=f32
+            taps_of(la_ref.at[frame], le_ref.at[frame]), weight, preferred_element_type=f32
         )
 
-    keep = inside(M2, 1)
+    a, b = origin()
+    position = place((M2, 1), 0)
+    core = position < CORE
+    row = jnp.where(core, (position * 2731) >> 16, (position - CORE) >> 1) + a * HL - 1
+    column = jnp.where(core, 0, b * WL - 1 + 25 * (position & 1))
+    keep = (row >= 0) & (row < GRID * HL) & (column >= 0) & (column < GRID * WL)
     for t in range(3):
-        act_ref[t, 0:M2, :] = jnp.where(keep, acc_ref[:, t * C : (t + 1) * C], 0.0)
-        spread(act_ref.at[t], M2, lh_ref.at[t])
+        for l in range(3):
+            act, rim = act_ref.at[t], rim_ref.at[t]
+            field = jnp.where(keep, acc_ref[:, lanes(l, t * C)], 0.0)
+            for y in range(10):
+                act[l, pl.ds(y * S + 1, WL), :] = field[y * WL : (y + 1) * WL]
+            rim[l] = field[CORE:M2]
+            for s in range(2):
+                act[l, pl.ds(25 * s, 10, stride=S), :] = rim[l, pl.ds(s, 10, stride=2), :]
+            for dx in range(3):
+                for y in range(0, 10, 2):
+                    lh_ref[t, y * WL : (y + 2) * WL, lanes(l, dx * C)] = strip(act, l, y * S + dx, 2).astype(bf16)
     for py in range(2):
         for px in range(2):
             lhs = jnp.concatenate(
                 [
                     jnp.concatenate(
                         [
-                            lh_ref[t, (py + ey) * S : (py + ey) * S + M3, (px + ex) * C : (px + ex + 1) * C]
+                            lh_ref[t, (py + ey) * WL : (py + ey) * WL + M3, (px + ex) * C : (px + ex + 1) * C]
                             for t in range(3)
                         ],
                         axis=0,
@@ -224,7 +279,7 @@
             phase = jnp.dot(lhs, tu_ref[py * 2 + px], preferred_element_type=f32) + bu
             for t in range(3):
                 for y in range(HL):
-                    row = t * M3 + y * S
+                    row = t * M3 + y * WL
                     for side in range(2):
                         up_ref[t, side, 2 * y + py, pl.ds(px, WL, stride=2), :] = phase[
                             row : row + WL, side * 128 : (side + 1) * 128
@@ -259,7 +314,7 @@
     acc4, tu, w2 = pl.pallas_call(
         front,
         out_shape=[
-            jax.ShapeDtypeStruct((M2, C), f32),
+            jax.ShapeDtypeStruct((3, 10 * S, 128), f32),
             jax.ShapeDtypeStruct((4, 4 * C, 256), bf16),
             pltpu.VMEM((3, 9 * C, C), bf16),
         ],
@@ -287,10 +342,12 @@
             pltpu.SemaphoreType.DMA((3,)),
             pltpu.VMEM((M0 + 8, 128), f32),
             pltpu.VMEM((2, M0, 256), bf16),
-            pltpu.VMEM((4, M1 + 8, C), f32),
-            pltpu.VMEM((4, M1, 3 * C), bf16),
+            pltpu.VMEM((4, 3, M1, 128), f32),
+            pltpu.VMEM((4, 30, EDGES, 128), f32),
+            pltpu.VMEM((4, 12 * WL, 3 * C), bf16),
+            pltpu.VMEM((4, EDGES, 9 * C), bf16),
             pltpu.VMEM((M2, 3 * C), f32),
-            pltpu.VMEM((3, M2, 3 * C), bf16),
+            pltpu.VMEM((3, CORE, 3 * C), bf16),
             pltpu.VMEM((3, 2, 2 * HL, 2 * WL, 128), f32),
             pltpu.VMEM((3, 1, 2 * HL, 2 * WL, C_UP), bf16),
         ],

time: 48.9 us -> 47.8 us (0.978)
  Pallas kernels: 19.4 us -> 18.3 us
    pallas_call x1, Pallas kernels: 14.8 us -> 13.7 us  [on_device(): pl.pallas_call(back, out_shape=jax.ShapeDtypeStruct((3, 1, 2 * HL, 2 * WL...]
where the time goes in v4:
time: 47.8 us; the launch traced here: 47.6 us
  blocking collectives  23.5 us (49%)
  Pallas kernels  18.3 us (38%)
  starting transfers between devices  3.14 us (7%)
  local copies, waits for them, and re-layouts  1.77 us (4%)
  other arithmetic  0.57 us (1%)
    all_to_all x1, blocking collectives, gather(): lax.all_to_all(pieces, 'tile', split_axis=0, concat_axis=0, tiled=True)  23.5 us
    pallas_call x1, Pallas kernels, on_device(): pl.pallas_call(back, out_shape=jax.ShapeDtypeStruct((3, 1, 2 * HL, 2 * WL...  13.7 us
    pallas_call x1, Pallas kernels, on_device(): pl.pallas_call(front, out_shape=[jax.ShapeDtypeStruct((3, 10 * S, 128), f...  3.95 us
    ppermute x1, starting transfers between devices, on_device(): lax.ppermute(last, 'tm', [(i, (i + 2) % count) for i in range(count)])  2.83 us
    reshape x2, local copies, waits for them, and re-layouts, gather(): tiles = latent.reshape(3, 3, GRID, GRID, LAT_C).transpose(2, 3, 1, 0, 4)  1.14 us
  transfers between devices with their start and end apart: 2, of which 0 were waited for; matrix products, arithmetic and copies ran while one was open for 0% of the time, Pallas kernels for 8%

profile of v4, /device:TPU:1, one launch (start us, length us, event | category | flops | bytes accessed | tf_op | source)
XLA Modules:
  0.0 47.6 jit_solution(12492345035667136889)
XLA Ops:
  0.0 0.0 copy-start.4
  0.0 0.0 copy-start.3
  0.0 0.0 copy-start.2
  0.0 0.0 copy-start
  0.0 0.0 copy-start.1
  0.0 1.0 %reshape.62 = bf16[3,3,8,8,16]{4,3,2,1,0:T(8,128)(2,1)S(1)} reshape(bf16[3,3,1024]{2,1,0:T(4,128)(2,1)} %param.8) | data formatting | bytes 36864 | tf_op jit(solution)/shard_map/reshape | solution.py:24
  1.1 0.1 copy.17
  1.2 0.1 slice.44
  1.3 0.3 pad_maximum_fusion
  1.6 0.2 reshape.63
  1.8 0.2 concatenate.39
  2.0 0.1 fusion.7
  2.1 0.1 fusion.3
  2.2 0.1 pad_maximum_fusion.1
  2.3 0.1 copy.15
  2.4 23.5 %all_to_all.5 = bf16[64,2,384]{2,1,0:T(2,128)(2,1)S(1)} all-to-all(bf16[64,2,384]{2,1,0:T(2,128)(2,1)S(1)} %copy.15), channel_id=1, replica_groups=mesh['tile'=64,'tm'=4] {'tile'}, dimensions={0} | all-to-all | bytes 196608 | tf_op jit(solution)/shard_map/all_to_all | solution.py:32
  26.0 0.6 %assemble.1 = (bf16[224,128]{1,0:T(8,128)(2,1)S(1)}, bf16[56,128]{1,0:T(8,128)(2,1)S(1)}) custom-call(bf16[128,384]{1,0:T(8,128)(2,1)S(1)} %reshape.64.pieces_ref), custom_call_target="tpu_custom_call" | custom-call | flops 100000000 | bytes 1000000 | tf_op jit(solution)/shard_map/assemble/pallas_call | solution.py:302
  26.6 2.8 %collective-permute-start.1 = (bf16[56,128]{1,0:T(8,128)(2,1)S(1)}, bf16[56,128]{1,0:T(8,128)(2,1)S(1)}, u32[]{:S(2)}, u32[]{:S(2)}) collective-permute-start(bf16[56,128]{1,0:T(8,128)(2,1)S(1)} %get-tuple-element.11), channel_id=1, source_target_pairs={{0,2},{1,3},{2,0},{3,1},{4,6},{5,7},{6,4},{7,5},{8,10},{9,11},{10,... | collective-permute-start | bytes 43016 | tf_op jit(solution)/shard_map/ppermute | solution.py:313
  29.5 0.3 collective-permute-start
  29.8 0.0 copy-done.4
  29.8 0.0 copy-done.3
  29.8 0.0 copy-done.2
  29.8 0.0 copy-done
  29.8 0.0 copy-done.1
  29.8 0.0 copy-start.5
  29.8 3.9 %front.1 = (f32[3,320,128]{2,1,0:T(8,128)S(1)}, bf16[4,1536,256]{2,1,0:T(8,128)(2,1)S(1)}, bf16[3,3456,384]{2,1,0:T(8,128)(2,1)S(1)}) custom-call(bf16[224,128]{1,0:T(8,128)(2,1)S(1)} %get-tuple-element.10.own_ref, bf16[432,384]{1,0:T(8,128)(2,1)S(1)} %bitcast.20, bf16[9,192,384]{2,1,0:T(8,128)(2,1)S(1)} %bitcast.19, bf16[3,3456,384]{2,1,0:T(8,128)(2,1)} %bitcast.22, ...), custom_call_target="tpu_custom_call" | custom-call | flops 1000000000 | bytes 10000000 | tf_op jit(solution)/shard_map/front/pallas_call | solution.py:314
  33.8 0.0 collective-permute-done.1.older_ref
  33.8 0.0 collective-permute-done.before_ref
  33.8 0.0 copy-done.5
  33.8 13.7 %back.1 = bf16[3,1,16,48,192]{4,3,2,1,0:T(8,128)(2,1)} custom-call(bf16[224,128]{1,0:T(8,128)(2,1)S(1)} %get-tuple-element.10.own_ref, bf16[224,128]{1,0:T(8,128)(2,1)S(1)} %collective-permute-done.before_ref, bf16[56,128]{1,0:T(8,128)(2,1)S(1)} %collective-permute-done.1.older_ref, f32[3,320,128]{2,1,0:T(8,128)S(1)} %get-tuple-element.12.acc4_ref, ...), custom_call_target="tpu_custom_call" | custom-call | flops 8000000000 | bytes 12000000 | tf_op jit(solution)/shard_map/back/pallas_call | solution.py:335
  (5 shorter events, 0.1 us)
Async XLA Ops:
  0.0 29.8 %copy-start.4 = (f32[384]{0:T(512)S(1)}, f32[384]{0:T(512)}, u32[]{:S(2)}) copy-start(f32[384]{0:T(512)} %b2_ref.3) | copy-start | bytes 4612
  0.0 29.8 %copy-start.3 = (f32[384]{0:T(512)S(1)}, f32[384]{0:T(512)}, u32[]{:S(2)}) copy-start(f32[384]{0:T(512)} %gain_ref.3) | copy-start | bytes 4612
  0.0 29.8 %copy-start.2 = (f32[384]{0:T(512)S(1)}, f32[384]{0:T(512)}, u32[]{:S(2)}) copy-start(f32[384]{0:T(512)} %b1_ref.3) | copy-start | bytes 4612
  0.0 29.8 %copy-start = (bf16[3,3,384,192]{2,3,1,0:T(8,128)(2,1)S(1)}, bf16[3,3,384,192]{2,3,1,0:T(8,128)(2,1)}, u32[]{:S(2)}) copy-start(bf16[3,3,384,192]{2,3,1,0:T(8,128)(2,1)} %param.14) | copy-start | bytes 3981316
  0.0 29.8 %copy-start.1 = (bf16[3,3,3,16,384]{4,3,2,1,0:T(8,128)(2,1)S(1)}, bf16[3,3,3,16,384]{4,3,2,1,0:T(8,128)(2,1)}, u32[]{:S(2)}) copy-start(bf16[3,3,3,16,384]{4,3,2,1,0:T(8,128)(2,1)} %param.9) | copy-start | bytes 995332
  26.6 7.1 %collective-permute-start.1 = (bf16[56,128]{1,0:T(8,128)(2,1)S(1)}, bf16[56,128]{1,0:T(8,128)(2,1)S(1)}, u32[]{:S(2)}, u32[]{:S(2)}) collective-permute-start(bf16[56,128]{1,0:T(8,128)(2,1)S(1)} %get-tuple-element.11), channel_id=1, source_target_pairs={{0,2},{1,3},{2,0},{3,1},{4,6},{5,7},{6,4},{7,5},{8,10},{9,11},{10,... | collective-permute-start | bytes 43016 | tf_op jit(solution)/shard_map/ppermute | solution.py:313
  29.5 4.3 %collective-permute-start = (bf16[224,128]{1,0:T(8,128)(2,1)S(1)}, bf16[224,128]{1,0:T(8,128)(2,1)S(1)}, u32[]{:S(2)}, u32[]{:S(2)}) collective-permute-start(bf16[224,128]{1,0:T(8,128)(2,1)S(1)} %get-tuple-element.10.own_ref), channel_id=1, source_target_pairs={{0,1},{1,2},{2,3},{3,0},{4,5},{5,6},{6,7},{7,4},{8,9},{9,10},{10,1... | collective-permute-start | bytes 172040 | tf_op jit(solution)/shard_map/ppermute | solution.py:312
  29.8 4.0 %copy-start.5 = (f32[192]{0:T(256)S(1)}, f32[192]{0:T(256)}, u32[]{:S(2)}) copy-start(f32[192]{0:T(256)} %bu_ref.1) | copy-start | bytes 2308

commit v5 on v4

--- a/solution.py
+++ b/solution.py
@@ -21,14 +21,21 @@
 
 
 def gather(latent):
-    tiles = latent.reshape(3, 3, GRID, GRID, LAT_C).transpose(2, 3, 1, 0, 4)
-    tiles = jnp.concatenate([tiles, tiles[:, :, :, 2:]], axis=3).reshape(GRID, GRID, 3 * 64)
-    index = lax.axis_index("tile")
-    r, g = index // GRID, index % GRID
-    side = jnp.where(g < 4, jnp.roll(tiles, -1, axis=1), jnp.roll(tiles, 1, axis=1))
-    wide = jnp.concatenate([tiles, side], axis=2)
-    other = jnp.where(r < 4, jnp.roll(wide, -1, axis=0), jnp.roll(wide, 1, axis=0))
-    pieces = jnp.stack([wide, other], axis=2).reshape(GRID * GRID, 2, 6 * 64)
+    pieces = pl.pallas_call(
+        deal,
+        out_shape=jax.ShapeDtypeStruct((2 * GRID * GRID, 6 * 64), bf16),
+        in_specs=[HBM],
+        out_specs=VMEM,
+        scratch_shapes=[
+            pltpu.VMEM(latent.shape, bf16),
+            pltpu.VMEM((3, 2 * GRID * GRID, 128), f32),
+            pltpu.SemaphoreType.DMA,
+        ],
+        compiler_params=pltpu.CompilerParams(vmem_limit_bytes=8 * 2**20),
+        cost_estimate=pl.CostEstimate(flops=10**9, bytes_accessed=10**7, transcendentals=0),
+        name="deal",
+    )(pltpu.with_memory_space_constraint(latent, pltpu.HBM))
+    pieces = pieces.reshape(GRID * GRID, 2, 6 * 64)
     own = lax.all_to_all(pieces, "tile", split_axis=0, concat_axis=0, tiled=True)
     return own.reshape(GRID * GRID * 2, 6 * 64)
 
@@ -40,6 +47,56 @@
 def origin():
     tile = lax.axis_index("tile")
     return lax.div(tile, GRID), lax.rem(tile, GRID)
+
+
+def deal(latent_hbm, out_ref, latent_ref, rows_ref, sem):
+    load = pltpu.make_async_copy(latent_hbm, latent_ref, sem)
+    load.start()
+    r, g = origin()
+    source, target = place((3 * 128, 128), 0), place((3 * 128, 128), 1)
+    frame = jnp.minimum(target >> 4, 2)
+    fold = ((source >> 7) == frame) & ((source & 15) == (target & 15)) & (target < 64)
+    fold = jnp.where(fold, 1.0, 0.0).astype(bf16)
+    load.wait()
+    own = (place((GRID, 128), 1) >> 4) == place((GRID, 128), 0)
+    spread = []
+    for cell in range(3):
+        blocks = []
+        for frame in range(3):
+            row = latent_ref[frame, pl.ds(cell, 1), :].astype(f32)
+            blocks.append(
+                jnp.concatenate(
+                    [
+                        jnp.where(own, jnp.broadcast_to(row[:, a * 128 : (a + 1) * 128], (GRID, 128)), 0.0)
+                        for a in range(GRID)
+                    ],
+                    axis=0,
+                )
+            )
+        spread.append(jnp.concatenate(blocks, axis=1))
+    spread = jnp.concatenate(spread, axis=0).astype(bf16)
+    cells = jnp.dot(spread, fold, preferred_element_type=f32)
+    count = GRID * GRID
+    cells = [cells[cell * count : (cell + 1) * count] for cell in range(3)]
+    sides = [
+        jnp.concatenate(
+            [
+                jnp.where(g < 4, pltpu.roll(row, 7, 0), pltpu.roll(row, 1, 0))
+                for row in (field[a * GRID : (a + 1) * GRID] for a in range(GRID))
+            ],
+            axis=0,
+        )
+        for field in cells
+    ]
+    groups = cells + sides
+    low = place((count, 128), 1) < 64
+    for j in range(3):
+        wide = jnp.where(low, groups[2 * j], pltpu.roll(groups[2 * j + 1], 64, 1))
+        above = jnp.concatenate([wide[GRID:], wide[:GRID]], axis=0)
+        below = jnp.concatenate([wide[-GRID:], wide[:-GRID]], axis=0)
+        rows_ref[j, pl.ds(0, count, stride=2), :] = wide
+        rows_ref[j, pl.ds(1, count, stride=2), :] = jnp.where(r < 4, above, below)
+        out_ref[:, j * 128 : (j + 1) * 128] = rows_ref[j].astype(bf16)
 
 
 def inside(rows, margin):

time: 47.8 us -> 46.6 us (0.975)
  local copies, waits for them, and re-layouts: 1.77 us -> 0.11 us
  Pallas kernels: 18.3 us -> 19.4 us
  other arithmetic: 0.57 us -> 0 us
    reshape x3 -> x1, local copies, waits for them, and re-layouts: 1.3 us -> 0.04 us  [gather(): pieces = pieces.reshape(GRID * GRID, 2, 6 * 64)]
    pallas_call x0 -> x1, Pallas kernels: none -> 1.15 us  [gather(): pl.pallas_call(deal, out_shape=jax.ShapeDtypeStruct((2 * GRID * GRID, 6 *...]
  transfers between devices with their start and end apart: 2 -> 2, of which waited for: 0 -> 0; matrix products, arithmetic and copies ran while one was open for 0% -> 0% of each run, Pallas kernels for 8% -> 9%
where the time goes in v5:
time: 46.6 us; the launch traced here: 46.4 us
  blocking collectives  23.5 us (50%)
  Pallas kernels  19.4 us (42%)
  starting transfers between devices  3.14 us (7%)
    all_to_all x1, blocking collectives, gather(): lax.all_to_all(pieces, 'tile', split_axis=0, concat_axis=0, tiled=True)  23.5 us
    pallas_call x1, Pallas kernels, on_device(): pl.pallas_call(back, out_shape=jax.ShapeDtypeStruct((3, 1, 2 * HL, 2 * WL...  13.7 us
    pallas_call x1, Pallas kernels, on_device(): pl.pallas_call(front, out_shape=[jax.ShapeDtypeStruct((3, 10 * S, 128), f...  3.95 us
    ppermute x1, starting transfers between devices, on_device(): lax.ppermute(last, 'tm', [(i, (i + 2) % count) for i in range(count)])  2.83 us
    pallas_call x1, Pallas kernels, gather(): pl.pallas_call(deal, out_shape=jax.ShapeDtypeStruct((2 * GRID * GRID, 6 *...  1.15 us
  transfers between devices with their start and end apart: 2, of which 0 were waited for; matrix products, arithmetic and copies ran while one was open for 0% of the time, Pallas kernels for 9%

profile of v5, /device:TPU:1, one launch (start us, length us, event | category | flops | bytes accessed | tf_op | source)
XLA Modules:
  0.0 46.4 jit_solution(9473514672346755773)
XLA Ops:
  0.0 0.0 copy-start.4
  0.0 0.0 copy-start.3
  0.0 0.0 copy-start.2
  0.0 0.0 copy-start
  0.0 0.0 copy-start.1
  0.0 1.1 %deal.1 = bf16[128,384]{1,0:T(8,128)(2,1)S(1)} custom-call(bf16[3,3,1024]{2,1,0:T(4,128)(2,1)} %latent_hbm.1), custom_call_target="tpu_custom_call" | custom-call | flops 1000000000 | bytes 10000000 | tf_op jit(solution)/shard_map/deal/pallas_call | solution.py:24
  1.2 23.5 %all_to_all.5 = bf16[64,2,384]{2,1,0:T(2,128)(2,1)S(1)} all-to-all(bf16[64,2,384]{2,1,0:T(2,128)(2,1)S(1)} %reshape.15), channel_id=1, replica_groups=mesh['tile'=64,'tm'=4] {'tile'}, dimensions={0} | all-to-all | bytes 196608 | tf_op jit(solution)/shard_map/all_to_all | solution.py:39
  24.8 0.6 %assemble.1 = (bf16[224,128]{1,0:T(8,128)(2,1)S(1)}, bf16[56,128]{1,0:T(8,128)(2,1)S(1)}) custom-call(bf16[128,384]{1,0:T(8,128)(2,1)S(1)} %reshape.16.pieces_ref), custom_call_target="tpu_custom_call" | custom-call | flops 100000000 | bytes 1000000 | tf_op jit(solution)/shard_map/assemble/pallas_call | solution.py:359
  25.4 2.8 %collective-permute-start.1 = (bf16[56,128]{1,0:T(8,128)(2,1)S(1)}, bf16[56,128]{1,0:T(8,128)(2,1)S(1)}, u32[]{:S(2)}, u32[]{:S(2)}) collective-permute-start(bf16[56,128]{1,0:T(8,128)(2,1)S(1)} %get-tuple-element.11), channel_id=1, source_target_pairs={{0,2},{1,3},{2,0},{3,1},{4,6},{5,7},{6,4},{7,5},{8,10},{9,11},{10,... | collective-permute-start | bytes 43016 | tf_op jit(solution)/shard_map/ppermute | solution.py:370
  28.3 0.3 collective-permute-start
  28.6 0.0 copy-done.4
  28.6 0.0 copy-done.3
  28.6 0.0 copy-done.2
  28.6 0.0 copy-done
  28.6 0.0 copy-done.1
  28.6 0.0 copy-start.5
  28.6 3.9 %front.1 = (f32[3,320,128]{2,1,0:T(8,128)S(1)}, bf16[4,1536,256]{2,1,0:T(8,128)(2,1)S(1)}, bf16[3,3456,384]{2,1,0:T(8,128)(2,1)S(1)}) custom-call(bf16[224,128]{1,0:T(8,128)(2,1)S(1)} %get-tuple-element.10.own_ref, bf16[432,384]{1,0:T(8,128)(2,1)S(1)} %bitcast.6, bf16[9,192,384]{2,1,0:T(8,128)(2,1)S(1)} %bitcast.5, bf16[3,3456,384]{2,1,0:T(8,128)(2,1)} %bitcast.8, ...), custom_call_target="tpu_custom_call" | custom-call | flops 1000000000 | bytes 10000000 | tf_op jit(solution)/shard_map/front/pallas_call | solution.py:371
  32.6 0.0 collective-permute-done.1.older_ref
  32.6 0.0 collective-permute-done.before_ref
  32.6 0.0 copy-done.5
  32.6 13.7 %back.1 = bf16[3,1,16,48,192]{4,3,2,1,0:T(8,128)(2,1)} custom-call(bf16[224,128]{1,0:T(8,128)(2,1)S(1)} %get-tuple-element.10.own_ref, bf16[224,128]{1,0:T(8,128)(2,1)S(1)} %collective-permute-done.before_ref, bf16[56,128]{1,0:T(8,128)(2,1)S(1)} %collective-permute-done.1.older_ref, f32[3,320,128]{2,1,0:T(8,128)S(1)} %get-tuple-element.12.acc4_ref, ...), custom_call_target="tpu_custom_call" | custom-call | flops 8000000000 | bytes 12000000 | tf_op jit(solution)/shard_map/back/pallas_call | solution.py:392
  (2 shorter events, 0.1 us)
Async XLA Ops:
  0.0 28.6 %copy-start.4 = (f32[384]{0:T(512)S(1)}, f32[384]{0:T(512)}, u32[]{:S(2)}) copy-start(f32[384]{0:T(512)} %b2_ref.3) | copy-start | bytes 4612
  0.0 28.6 %copy-start.3 = (f32[384]{0:T(512)S(1)}, f32[384]{0:T(512)}, u32[]{:S(2)}) copy-start(f32[384]{0:T(512)} %gain_ref.3) | copy-start | bytes 4612
  0.0 28.6 %copy-start.2 = (f32[384]{0:T(512)S(1)}, f32[384]{0:T(512)}, u32[]{:S(2)}) copy-start(f32[384]{0:T(512)} %b1_ref.3) | copy-start | bytes 4612
  0.0 28.6 %copy-start = (bf16[3,3,384,192]{2,3,1,0:T(8,128)(2,1)S(1)}, bf16[3,3,384,192]{2,3,1,0:T(8,128)(2,1)}, u32[]{:S(2)}) copy-start(bf16[3,3,384,192]{2,3,1,0:T(8,128)(2,1)} %param.14) | copy-start | bytes 3981316
  0.0 28.6 %copy-start.1 = (bf16[3,3,3,16,384]{4,3,2,1,0:T(8,128)(2,1)S(1)}, bf16[3,3,3,16,384]{4,3,2,1,0:T(8,128)(2,1)}, u32[]{:S(2)}) copy-start(bf16[3,3,3,16,384]{4,3,2,1,0:T(8,128)(2,1)} %param.9) | copy-start | bytes 995332
  25.4 7.1 %collective-permute-start.1 = (bf16[56,128]{1,0:T(8,128)(2,1)S(1)}, bf16[56,128]{1,0:T(8,128)(2,1)S(1)}, u32[]{:S(2)}, u32[]{:S(2)}) collective-permute-start(bf16[56,128]{1,0:T(8,128)(2,1)S(1)} %get-tuple-element.11), channel_id=1, source_target_pairs={{0,2},{1,3},{2,0},{3,1},{4,6},{5,7},{6,4},{7,5},{8,10},{9,11},{10,... | collective-permute-start | bytes 43016 | tf_op jit(solution)/shard_map/ppermute | solution.py:370
  28.3 4.3 %collective-permute-start = (bf16[224,128]{1,0:T(8,128)(2,1)S(1)}, bf16[224,128]{1,0:T(8,128)(2,1)S(1)}, u32[]{:S(2)}, u32[]{:S(2)}) collective-permute-start(bf16[224,128]{1,0:T(8,128)(2,1)S(1)} %get-tuple-element.10.own_ref), channel_id=1, source_target_pairs={{0,1},{1,2},{2,3},{3,0},{4,5},{5,6},{6,7},{7,4},{8,9},{9,10},{10,1... | collective-permute-start | bytes 172040 | tf_op jit(solution)/shard_map/ppermute | solution.py:369
  28.6 4.0 %copy-start.5 = (f32[192]{0:T(256)S(1)}, f32[192]{0:T(256)}, u32[]{:S(2)}) copy-start(f32[192]{0:T(256)} %bu_ref.1) | copy-start | bytes 2308

commit v6 on v5

--- a/solution.py
+++ b/solution.py
@@ -14,6 +14,7 @@
 S = 32
 M0, M1 = 14 * S, 12 * S
 EDGES = 24
+RIM, TALL = 32, 18 * S
 CORE, M2, M3 = 10 * WL, 10 * WL + EDGES, HL * WL
 bf16, f32 = jnp.bfloat16, jnp.float32
 VMEM = pl.BlockSpec(memory_space=pltpu.VMEM)
@@ -175,7 +176,7 @@
 def edge(ref, l, first, rim_ref):
     for s in range(2):
         rim_ref[pl.ds(s, 10, stride=2), :] = ref[l, pl.ds(first + 25 * s, 10, stride=S), :]
-    return rim_ref[...]
+    return rim_ref[0:EDGES, :]
 
 
 def silu_of_norm(start, gain):
@@ -186,7 +187,7 @@
 
 def residual(start, b2, act_ref, rim_ref, target, first):
     for l in range(3):
-        act_ref[l] = start[:, lanes(l)]
+        act_ref[l, 0:M1, :] = start[:, lanes(l)]
         target[0:CORE, lanes(l, first)] = strip(act_ref, l, S + 2, 10) + b2[:, lanes(l)]
         target[CORE:M2, lanes(l, first)] = edge(act_ref, l, S + 1, rim_ref.at[27 + l]) + b2[:, lanes(l)]
 
@@ -194,7 +195,7 @@
 def activate(start, gain, keep, act_ref, rim_ref, la_ref, le_ref):
     value = jnp.where(keep, silu_of_norm(start, gain), 0.0)
     for l in range(3):
-        act_ref[l] = value[:, lanes(l)]
+        act_ref[l, 0:M1, :] = value[:, lanes(l)]
         for dx in range(3):
             for y in range(0, 12, 2):
                 la_ref[y * WL : (y + 2) * WL, lanes(l, dx * C)] = strip(act_ref, l, y * S + 1 + dx, 2).astype(bf16)
@@ -247,7 +248,7 @@
     loads[0].wait()
     field = kept + jnp.dot(rows_of(la_ref, 10 * S), w2_ref[2], preferred_element_type=f32)
     for l in range(3):
-        acc_ref[l] = field[:, lanes(l)]
+        acc_ref[l, 0 : 10 * S, :] = field[:, lanes(l)]
     for load in loads[1:]:
         load.wait()
 
@@ -311,7 +312,7 @@
             field = jnp.where(keep, acc_ref[:, lanes(l, t * C)], 0.0)
             for y in range(10):
                 act[l, pl.ds(y * S + 1, WL), :] = field[y * WL : (y + 1) * WL]
-            rim[l] = field[CORE:M2]
+            rim[l, 0:EDGES, :] = field[CORE:M2]
             for s in range(2):
                 act[l, pl.ds(25 * s, 10, stride=S), :] = rim[l, pl.ds(s, 10, stride=2), :]
             for dx in range(3):
@@ -371,7 +372,7 @@
     acc4, tu, w2 = pl.pallas_call(
         front,
         out_shape=[
-            jax.ShapeDtypeStruct((3, 10 * S, 128), f32),
+            jax.ShapeDtypeStruct((3, 16 * S, 128), f32),
             jax.ShapeDtypeStruct((4, 4 * C, 256), bf16),
             pltpu.VMEM((3, 9 * C, C), bf16),
         ],
@@ -399,8 +400,8 @@
             pltpu.SemaphoreType.DMA((3,)),
             pltpu.VMEM((M0 + 8, 128), f32),
             pltpu.VMEM((2, M0, 256), bf16),
-            pltpu.VMEM((4, 3, M1, 128), f32),
-            pltpu.VMEM((4, 30, EDGES, 128), f32),
+            pltpu.VMEM((4, 3, TALL, 128), f32),
+            pltpu.VMEM((4, 30, RIM, 128), f32),
             pltpu.VMEM((4, 12 * WL, 3 * C), bf16),
             pltpu.VMEM((4, EDGES, 9 * C), bf16),
             pltpu.VMEM((M2, 3 * C), f32),

time: 46.6 us -> 46.6 us (level)
  transfers between devices with their start and end apart: 2 -> 2, of which waited for: 0 -> 0; matrix products, arithmetic and copies ran while one was open for 0% -> 0% of each run, Pallas kernels for 9% -> 8%
where the time goes in v6:
time: 46.6 us; the launch traced here: 46.5 us
  blocking collectives  23.5 us (50%)
  Pallas kernels  19.4 us (42%)
  starting transfers between devices  3.14 us (7%)
    all_to_all x1, blocking collectives, gather(): lax.all_to_all(pieces, 'tile', split_axis=0, concat_axis=0, tiled=True)  23.5 us
    pallas_call x1, Pallas kernels, on_device(): pl.pallas_call(back, out_shape=jax.ShapeDtypeStruct((3, 1, 2 * HL, 2 * WL...  13.7 us
    pallas_call x1, Pallas kernels, on_device(): pl.pallas_call(front, out_shape=[jax.ShapeDtypeStruct((3, 16 * S, 128), f...  3.95 us
    ppermute x1, starting transfers between devices, on_device(): lax.ppermute(last, 'tm', [(i, (i + 2) % count) for i in range(count)])  2.83 us
    pallas_call x1, Pallas kernels, gather(): pl.pallas_call(deal, out_shape=jax.ShapeDtypeStruct((2 * GRID * GRID, 6 *...  1.15 us
  transfers between devices with their start and end apart: 2, of which 0 were waited for; matrix products, arithmetic and copies ran while one was open for 0% of the time, Pallas kernels for 8%

profile of v6, /device:TPU:1, one launch (start us, length us, event | category | flops | bytes accessed | tf_op | source)
XLA Modules:
  0.0 46.5 jit_solution(12033351104108432589)
XLA Ops:
  0.0 0.0 copy-start.4
  0.0 0.0 copy-start.3
  0.0 0.0 copy-start.2
  0.0 0.0 copy-start
  0.0 0.0 copy-start.1
  0.0 1.1 %deal.1 = bf16[128,384]{1,0:T(8,128)(2,1)S(1)} custom-call(bf16[3,3,1024]{2,1,0:T(4,128)(2,1)} %latent_hbm.1), custom_call_target="tpu_custom_call" | custom-call | flops 1000000000 | bytes 10000000 | tf_op jit(solution)/shard_map/deal/pallas_call | solution.py:25
  1.2 23.5 %all_to_all.5 = bf16[64,2,384]{2,1,0:T(2,128)(2,1)S(1)} all-to-all(bf16[64,2,384]{2,1,0:T(2,128)(2,1)S(1)} %reshape.15), channel_id=1, replica_groups=mesh['tile'=64,'tm'=4] {'tile'}, dimensions={0} | all-to-all | bytes 196608 | tf_op jit(solution)/shard_map/all_to_all | solution.py:40
  24.8 0.6 %assemble.1 = (bf16[224,128]{1,0:T(8,128)(2,1)S(1)}, bf16[56,128]{1,0:T(8,128)(2,1)S(1)}) custom-call(bf16[128,384]{1,0:T(8,128)(2,1)S(1)} %reshape.16.pieces_ref), custom_call_target="tpu_custom_call" | custom-call | flops 100000000 | bytes 1000000 | tf_op jit(solution)/shard_map/assemble/pallas_call | solution.py:360
  25.4 2.8 %collective-permute-start.1 = (bf16[56,128]{1,0:T(8,128)(2,1)S(1)}, bf16[56,128]{1,0:T(8,128)(2,1)S(1)}, u32[]{:S(2)}, u32[]{:S(2)}) collective-permute-start(bf16[56,128]{1,0:T(8,128)(2,1)S(1)} %get-tuple-element.11), channel_id=1, source_target_pairs={{0,2},{1,3},{2,0},{3,1},{4,6},{5,7},{6,4},{7,5},{8,10},{9,11},{10,... | collective-permute-start | bytes 43016 | tf_op jit(solution)/shard_map/ppermute | solution.py:371
  28.3 0.3 collective-permute-start
  28.6 0.0 copy-done.4
  28.6 0.0 copy-done.3
  28.6 0.0 copy-done.2
  28.6 0.0 copy-done
  28.6 0.0 copy-done.1
  28.6 0.0 copy-start.5
  28.6 3.9 %front.1 = (f32[3,512,128]{2,1,0:T(8,128)S(1)}, bf16[4,1536,256]{2,1,0:T(8,128)(2,1)S(1)}, bf16[3,3456,384]{2,1,0:T(8,128)(2,1)S(1)}) custom-call(bf16[224,128]{1,0:T(8,128)(2,1)S(1)} %get-tuple-element.10.own_ref, bf16[432,384]{1,0:T(8,128)(2,1)S(1)} %bitcast.6, bf16[9,192,384]{2,1,0:T(8,128)(2,1)S(1)} %bitcast.5, bf16[3,3456,384]{2,1,0:T(8,128)(2,1)} %bitcast.8, ...), custom_call_target="tpu_custom_call" | custom-call | flops 1000000000 | bytes 10000000 | tf_op jit(solution)/shard_map/front/pallas_call | solution.py:372
  32.6 0.0 collective-permute-done.1.older_ref
  32.6 0.0 collective-permute-done.before_ref
  32.6 0.0 copy-done.5
  32.6 13.7 %back.1 = bf16[3,1,16,48,192]{4,3,2,1,0:T(8,128)(2,1)} custom-call(bf16[224,128]{1,0:T(8,128)(2,1)S(1)} %get-tuple-element.10.own_ref, bf16[224,128]{1,0:T(8,128)(2,1)S(1)} %collective-permute-done.before_ref, bf16[56,128]{1,0:T(8,128)(2,1)S(1)} %collective-permute-done.1.older_ref, f32[3,512,128]{2,1,0:T(8,128)S(1)} %get-tuple-element.12.acc4_ref, ...), custom_call_target="tpu_custom_call" | custom-call | flops 8000000000 | bytes 12000000 | tf_op jit(solution)/shard_map/back/pallas_call | solution.py:393
  (2 shorter events, 0.1 us)
Async XLA Ops:
  0.0 28.6 %copy-start.4 = (f32[384]{0:T(512)S(1)}, f32[384]{0:T(512)}, u32[]{:S(2)}) copy-start(f32[384]{0:T(512)} %b2_ref.3) | copy-start | bytes 4612
  0.0 28.6 %copy-start.3 = (f32[384]{0:T(512)S(1)}, f32[384]{0:T(512)}, u32[]{:S(2)}) copy-start(f32[384]{0:T(512)} %gain_ref.3) | copy-start | bytes 4612
  0.0 28.6 %copy-start.2 = (f32[384]{0:T(512)S(1)}, f32[384]{0:T(512)}, u32[]{:S(2)}) copy-start(f32[384]{0:T(512)} %b1_ref.3) | copy-start | bytes 4612
  0.0 28.6 %copy-start = (bf16[3,3,384,192]{2,3,1,0:T(8,128)(2,1)S(1)}, bf16[3,3,384,192]{2,3,1,0:T(8,128)(2,1)}, u32[]{:S(2)}) copy-start(bf16[3,3,384,192]{2,3,1,0:T(8,128)(2,1)} %param.14) | copy-start | bytes 3981316
  0.0 28.6 %copy-start.1 = (bf16[3,3,3,16,384]{4,3,2,1,0:T(8,128)(2,1)S(1)}, bf16[3,3,3,16,384]{4,3,2,1,0:T(8,128)(2,1)}, u32[]{:S(2)}) copy-start(bf16[3,3,3,16,384]{4,3,2,1,0:T(8,128)(2,1)} %param.9) | copy-start | bytes 995332
  25.4 7.1 %collective-permute-start.1 = (bf16[56,128]{1,0:T(8,128)(2,1)S(1)}, bf16[56,128]{1,0:T(8,128)(2,1)S(1)}, u32[]{:S(2)}, u32[]{:S(2)}) collective-permute-start(bf16[56,128]{1,0:T(8,128)(2,1)S(1)} %get-tuple-element.11), channel_id=1, source_target_pairs={{0,2},{1,3},{2,0},{3,1},{4,6},{5,7},{6,4},{7,5},{8,10},{9,11},{10,... | collective-permute-start | bytes 43016 | tf_op jit(solution)/shard_map/ppermute | solution.py:371
  28.3 4.3 %collective-permute-start = (bf16[224,128]{1,0:T(8,128)(2,1)S(1)}, bf16[224,128]{1,0:T(8,128)(2,1)S(1)}, u32[]{:S(2)}, u32[]{:S(2)}) collective-permute-start(bf16[224,128]{1,0:T(8,128)(2,1)S(1)} %get-tuple-element.10.own_ref), channel_id=1, source_target_pairs={{0,1},{1,2},{2,3},{3,0},{4,5},{5,6},{6,7},{7,4},{8,9},{9,10},{10,1... | collective-permute-start | bytes 172040 | tf_op jit(solution)/shard_map/ppermute | solution.py:370
  28.6 4.0 %copy-start.5 = (f32[192]{0:T(256)S(1)}, f32[192]{0:T(256)}, u32[]{:S(2)}) copy-start(f32[192]{0:T(256)} %bu_ref.1) | copy-start | bytes 2308
